TPU v7x, 32 devices: a whole 2x2x4 slice. The times are simulated.
32 devices in a mesh: segment: 4 (over y, x), graph: 8 (over z, core).
Axes of the slice: x: 2, y: 2, z: 4, core: 2. Of those that a mesh axis runs over, the one named last changes fastest.
Arguments:
- features: bfloat16 [4096, 1024], P('graph'), may hold values from -6 to 6
- weights: bfloat16 [8, 1024, 1024], P(None, 'graph'), may hold values from -0.25 to 0.25
- history: bfloat16 [8, 512, 1024], P(None, 'graph'), may hold values from 0 to 1.1953125
- own_adj: bfloat16 [4, 1024, 128], P(None, 'graph'), may hold values from 0 to 0.00390625
- side_adj: bfloat16 [4, 4, 128, 128], P(None, None, 'graph'), may hold values from 0 to 0.012451172
- hist_adj: bfloat16 [4, 512, 128], P(None, 'graph'), may hold values from 0 to 0.009338379
- send_ids: int32 [4, 4, 128], P(None, None, 'graph'), may hold values from 0 to 127, as said below
- hist_ids: int32 [4, 512], P(None, 'graph'), may hold values from 0 to 63
Outputs:
- layer_out: bfloat16 [8, 4096, 1024], P('segment', 'graph')
Inputs may be any that keep to these rules, and one draw needn't show every extreme that they name: `send_ids`: each list of 16 row numbers for one batch, one partition and one direction has distinct entries.
All inputs are finite; a program needn't handle non-finite values.
Results may differ from a plain program's by a relative error of at most 0.0032.
Values may be sent and summed in bfloat16 or wider, within the bound.
A program may use at most 64 MiB of HBM per device.

v0:
```python
import jax
import jax.numpy as jnp
from jax import lax
from jax.sharding import PartitionSpec as P

ALPHA = 0.1
LAMBDA = 1.5
OFFSETS = (1, -1, 2, -2)


def shifted(value, axis, steps):
    count = lax.axis_size(axis)
    initial, last = (max(0, -steps), min(count, count - steps))
    return lax.ppermute(value, axis, [(source, source + steps) for source in range(initial, last)])


def propagate(
    current, initial, layer_number, weight, tables, own_tile, side_tile, send_rows, past_rows
):
    edge_count = send_rows.shape[1]
    picked = jnp.take(current, send_rows.reshape(-1), axis=0)
    arrived = []
    for direction in range(len(OFFSETS)):
        outgoing = picked[direction * edge_count : (direction + 1) * edge_count]
        arrived.append(shifted(outgoing, "graph", OFFSETS[direction]))
    layer_table = lax.dynamic_index_in_dim(tables, layer_number, 0, keepdims=False)
    arrived.append(jnp.take(layer_table, past_rows, axis=0))
    gathered_rows = jnp.concatenate(arrived, axis=0)
    aggregate = jnp.dot(own_tile, current, preferred_element_type=jnp.float32)
    aggregate = aggregate + lax.dot_general(
        side_tile, gathered_rows, (((0,), (0,)), ((), ())), preferred_element_type=jnp.float32
    )
    support = (1.0 - ALPHA) * aggregate + ALPHA * initial.astype(jnp.float32)
    mixing = jnp.dot(support.astype(jnp.bfloat16), weight, preferred_element_type=jnp.float32)
    strength = jnp.log(LAMBDA / (layer_number.astype(jnp.float32) + 1.0) + 1.0)
    return jax.nn.relu((1.0 - strength) * support + strength * mixing).astype(jnp.bfloat16)


def batch_tiles(own_adj, side_adj, hist_adj, send_ids, hist_ids, batch_safe):
    batch_rows = own_adj.shape[2]
    side_edges = side_adj.shape[1] * side_adj.shape[2]
    own_tile = lax.dynamic_index_in_dim(own_adj, batch_safe, 0, keepdims=False)
    edge_tile = lax.dynamic_index_in_dim(side_adj, batch_safe, 0, keepdims=False).reshape(
        side_edges, batch_rows
    )
    past_tile = lax.dynamic_index_in_dim(hist_adj, batch_safe, 0, keepdims=False)
    side_tile = jnp.concatenate([edge_tile, past_tile], axis=0)
    send_rows = lax.dynamic_index_in_dim(send_ids, batch_safe, 0, keepdims=False)
    past_rows = lax.dynamic_index_in_dim(hist_ids, batch_safe, 0, keepdims=False)
    return (own_tile, side_tile, send_rows, past_rows)


def shards(features, weights, history, own_adj, side_adj, hist_adj, send_ids, hist_ids):
    segment_pos = lax.axis_index("segment")
    segment_count = lax.axis_size("segment")
    batch_count = own_adj.shape[0]
    batch_rows = own_adj.shape[2]
    layer_total = weights.shape[0]
    kept_slots = layer_total // segment_count
    initial = lax.dynamic_slice_in_dim(features, segment_pos * batch_rows, batch_rows, 0)
    own_tile, side_tile, send_rows, past_rows = batch_tiles(
        own_adj, side_adj, hist_adj, send_ids, hist_ids, segment_pos
    )
    current = initial
    produced = []
    for number in range(layer_total):
        weight = lax.all_gather(weights[number], "graph", axis=0, tiled=True)
        current = propagate(
            current,
            initial,
            jnp.int32(number),
            weight,
            history,
            own_tile,
            side_tile,
            send_rows,
            past_rows,
        )
        produced.append(current)
    arranged = jnp.stack(
        [
            jnp.stack([produced[kept_slots * target + slot] for target in range(segment_count)])
            for slot in range(kept_slots)
        ]
    )
    received = lax.all_to_all(arranged, "segment", split_axis=1, concat_axis=1, tiled=True)
    return received.reshape(kept_slots, batch_count * batch_rows, features.shape[1])


def solution(mesh):
    in_specs = (
        P("graph", None),
        P(None, "graph", None),
        P(None, "graph", None),
        P(None, "graph", None),
        P(None, None, "graph", None),
        P(None, "graph", None),
        P(None, None, "graph"),
        P(None, "graph"),
    )
    out_specs = P("segment", "graph", None)
    return jax.shard_map(shards, mesh=mesh, in_specs=in_specs, out_specs=out_specs, check_vma=False)
```

profile of v0, /device:TPU:6, one launch (start us, length us, event | category | flops | bytes accessed | tf_op | source)
XLA Modules:
  0.0 296.4 jit_solution(15457748566098443575)
XLA Ops:
  6.5 2.9 fusion.172
  15.8 2.3 collective-permute-start
  19.4 5.4 %collective-permute-start.2 = (bf16[16,1024]{1,0:T(8,128)(2,1)}, bf16[16,1024]{1,0:T(8,128)(2,1)S(1)}, u32[]{:S(2)}, u32[]{:S(2)}) collective-permute-start(bf16[16,1024]{1,0:T(8,128)(2,1)} %get-tuple-element.54), channel_id=1, source_target_pairs={{0,2},{1,3},{2,4},{3,5},{4,6},{5,7},{8,10},{9,11},{10,12},{11,13},... | collective-permute-start | bytes 98312 | tf_op jit(solution)/shard_map/ppermute | solution.py:14
  26.9 1.4 slice_bitcast_fusion
  30.0 1.3 gather_fusion.1
  34.9 1.4 gather_fusion.13
  36.2 1.4 gather_fusion.15
  38.8 2.2 all-gather.17.cloned.1.call-done
  41.0 2.1 fusion.125
  43.9 2.1 collective-permute-start.4
  47.5 5.5 %collective-permute-start.6 = (bf16[16,1024]{1,0:T(8,128)(2,1)S(1)}, bf16[16,1024]{1,0:T(8,128)(2,1)S(1)}, u32[]{:S(2)}, u32[]{:S(2)}) collective-permute-start(bf16[16,1024]{1,0:T(8,128)(2,1)S(1)} %get-tuple-element.50), channel_id=1, source_target_pairs={{0,2},{1,3},{2,4},{3,5},{4,6},{5,7},{8,10},{9,11},{10,12},{11,13},... | collective-permute-start | bytes 98312 | tf_op jit(solution)/shard_map/ppermute | solution.py:14
  55.1 5.0 %collective-permute-done.7 = bf16[16,1024]{1,0:T(8,128)(2,1)S(1)} collective-permute-done((bf16[16,1024]{1,0:T(8,128)(2,1)S(1)}, bf16[16,1024]{1,0:T(8,128)(2,1)S(1)}, u32[]{:S(2)}, u32[]{:S(2)}) %collective-permute-start.7) | collective-permute-done | bytes 32800 | tf_op jit(solution)/shard_map/ppermute | solution.py:14
  60.5 11.5 %all-gather.19.cloned.1.call-done = bf16[1,1024,1024]{2,1,0:T(8,128)(2,1)} async-done(((bf16[1,128,1024]{2,1,0:T(8,128)(2,1)}), bf16[1,1024,1024]{2,1,0:T(8,128)(2,1)}) %all-gather.19.cloned.1.call-update) | async-done | bytes 2097168 | tf_op jit(solution)/shard_map/all_gather | solution.py:67
  72.0 2.1 fusion.122
  74.9 2.1 collective-permute-start.8
  78.6 5.4 %collective-permute-start.10 = (bf16[16,1024]{1,0:T(8,128)(2,1)S(1)}, bf16[16,1024]{1,0:T(8,128)(2,1)S(1)}, u32[]{:S(2)}, u32[]{:S(2)}) collective-permute-start(bf16[16,1024]{1,0:T(8,128)(2,1)S(1)} %get-tuple-element.46), channel_id=1, source_target_pairs={{0,2},{1,3},{2,4},{3,5},{4,6},{5,7},{8,10},{9,11},{10,12},{11,13},... | collective-permute-start | bytes 98312 | tf_op jit(solution)/shard_map/ppermute | solution.py:14
  86.1 5.2 %collective-permute-done.11 = bf16[16,1024]{1,0:T(8,128)(2,1)S(1)} collective-permute-done((bf16[16,1024]{1,0:T(8,128)(2,1)S(1)}, bf16[16,1024]{1,0:T(8,128)(2,1)S(1)}, u32[]{:S(2)}, u32[]{:S(2)}) %collective-permute-start.11) | collective-permute-done | bytes 32800 | tf_op jit(solution)/shard_map/ppermute | solution.py:14
  91.6 11.4 %all-gather.21.cloned.1.call-done = bf16[1,1024,1024]{2,1,0:T(8,128)(2,1)} async-done(((bf16[1,128,1024]{2,1,0:T(8,128)(2,1)}), bf16[1,1024,1024]{2,1,0:T(8,128)(2,1)}) %all-gather.21.cloned.1.call-update) | async-done | bytes 2097168 | tf_op jit(solution)/shard_map/all_gather | solution.py:67
  103.0 2.1 fusion.119
  105.9 2.1 collective-permute-start.12
  109.5 5.4 %collective-permute-start.14 = (bf16[16,1024]{1,0:T(8,128)(2,1)S(1)}, bf16[16,1024]{1,0:T(8,128)(2,1)S(1)}, u32[]{:S(2)}, u32[]{:S(2)}) collective-permute-start(bf16[16,1024]{1,0:T(8,128)(2,1)S(1)} %get-tuple-element.42), channel_id=1, source_target_pairs={{0,2},{1,3},{2,4},{3,5},{4,6},{5,7},{8,10},{9,11},{10,12},{11,13},... | collective-permute-start | bytes 98312 | tf_op jit(solution)/shard_map/ppermute | solution.py:14
  117.0 5.1 %collective-permute-done.15 = bf16[16,1024]{1,0:T(8,128)(2,1)S(1)} collective-permute-done((bf16[16,1024]{1,0:T(8,128)(2,1)S(1)}, bf16[16,1024]{1,0:T(8,128)(2,1)S(1)}, u32[]{:S(2)}, u32[]{:S(2)}) %collective-permute-start.15) | collective-permute-done | bytes 32800 | tf_op jit(solution)/shard_map/ppermute | solution.py:14
  122.5 11.8 %all-gather.23.cloned.1.call-done = bf16[1,1024,1024]{2,1,0:T(8,128)(2,1)} async-done(((bf16[1,128,1024]{2,1,0:T(8,128)(2,1)}), bf16[1,1024,1024]{2,1,0:T(8,128)(2,1)}) %all-gather.23.cloned.1.call-update) | async-done | bytes 2097168 | tf_op jit(solution)/shard_map/all_gather | solution.py:67
  134.3 2.1 fusion.116
  137.2 2.1 collective-permute-start.16
  140.9 4.8 %collective-permute-start.18 = (bf16[16,1024]{1,0:T(8,128)(2,1)S(1)}, bf16[16,1024]{1,0:T(8,128)(2,1)S(1)}, u32[]{:S(2)}, u32[]{:S(2)}) collective-permute-start(bf16[16,1024]{1,0:T(8,128)(2,1)S(1)} %get-tuple-element.38), channel_id=1, source_target_pairs={{0,2},{1,3},{2,4},{3,5},{4,6},{5,7},{8,10},{9,11},{10,12},{11,13},... | collective-permute-start | bytes 98312 | tf_op jit(solution)/shard_map/ppermute | solution.py:14
  145.7 1.3 collective-permute-start.19
  147.8 5.1 %collective-permute-done.19 = bf16[16,1024]{1,0:T(8,128)(2,1)S(1)} collective-permute-done((bf16[16,1024]{1,0:T(8,128)(2,1)S(1)}, bf16[16,1024]{1,0:T(8,128)(2,1)S(1)}, u32[]{:S(2)}, u32[]{:S(2)}) %collective-permute-start.19) | collective-permute-done | bytes 32800 | tf_op jit(solution)/shard_map/ppermute | solution.py:14
  153.3 11.8 %all-gather.25.cloned.1.call-done = bf16[1,1024,1024]{2,1,0:T(8,128)(2,1)} async-done(((bf16[1,128,1024]{2,1,0:T(8,128)(2,1)}), bf16[1,1024,1024]{2,1,0:T(8,128)(2,1)}) %all-gather.25.cloned.1.call-update) | async-done | bytes 2097168 | tf_op jit(solution)/shard_map/all_gather | solution.py:67
  165.1 2.1 fusion.113
  168.0 2.1 collective-permute-start.20
  171.7 4.8 %collective-permute-start.22 = (bf16[16,1024]{1,0:T(8,128)(2,1)S(1)}, bf16[16,1024]{1,0:T(8,128)(2,1)S(1)}, u32[]{:S(2)}, u32[]{:S(2)}) collective-permute-start(bf16[16,1024]{1,0:T(8,128)(2,1)S(1)} %get-tuple-element.34), channel_id=1, source_target_pairs={{0,2},{1,3},{2,4},{3,5},{4,6},{5,7},{8,10},{9,11},{10,12},{11,13},... | collective-permute-start | bytes 98312 | tf_op jit(solution)/shard_map/ppermute | solution.py:14
  176.5 1.3 collective-permute-start.23
  178.6 5.1 %collective-permute-done.23 = bf16[16,1024]{1,0:T(8,128)(2,1)S(1)} collective-permute-done((bf16[16,1024]{1,0:T(8,128)(2,1)S(1)}, bf16[16,1024]{1,0:T(8,128)(2,1)S(1)}, u32[]{:S(2)}, u32[]{:S(2)}) %collective-permute-start.23) | collective-permute-done | bytes 32800 | tf_op jit(solution)/shard_map/ppermute | solution.py:14
  184.1 11.8 %all-gather.27.cloned.1.call-done = bf16[1,1024,1024]{2,1,0:T(8,128)(2,1)} async-done(((bf16[1,128,1024]{2,1,0:T(8,128)(2,1)}), bf16[1,1024,1024]{2,1,0:T(8,128)(2,1)}) %all-gather.27.cloned.1.call-update) | async-done | bytes 2097168 | tf_op jit(solution)/shard_map/all_gather | solution.py:67
  195.9 2.1 fusion.110
  198.8 2.1 collective-permute-start.24
  203.2 4.8 %collective-permute-start.26 = (bf16[16,1024]{1,0:T(8,128)(2,1)S(1)}, bf16[16,1024]{1,0:T(8,128)(2,1)S(1)}, u32[]{:S(2)}, u32[]{:S(2)}) collective-permute-start(bf16[16,1024]{1,0:T(8,128)(2,1)S(1)} %get-tuple-element.30), channel_id=1, source_target_pairs={{0,2},{1,3},{2,4},{3,5},{4,6},{5,7},{8,10},{9,11},{10,12},{11,13},... | collective-permute-start | bytes 98312 | tf_op jit(solution)/shard_map/ppermute | solution.py:14
  210.1 5.1 %collective-permute-done.27 = bf16[16,1024]{1,0:T(8,128)(2,1)S(1)} collective-permute-done((bf16[16,1024]{1,0:T(8,128)(2,1)S(1)}, bf16[16,1024]{1,0:T(8,128)(2,1)S(1)}, u32[]{:S(2)}, u32[]{:S(2)}) %collective-permute-start.27) | collective-permute-done | bytes 32800 | tf_op jit(solution)/shard_map/ppermute | solution.py:14
  216.4 10.6 %all-gather.29.cloned.1.call-done = bf16[1,1024,1024]{2,1,0:T(8,128)(2,1)} async-done(((bf16[1,128,1024]{2,1,0:T(8,128)(2,1)}), bf16[1,1024,1024]{2,1,0:T(8,128)(2,1)}) %all-gather.29.cloned.1.call-update) | async-done | bytes 2097168 | tf_op jit(solution)/shard_map/all_gather | solution.py:67
  227.0 2.3 fusion.107
  230.2 2.1 collective-permute-start.28
  233.6 4.6 %collective-permute-start.30 = (bf16[16,1024]{1,0:T(8,128)(2,1)S(1)}, bf16[16,1024]{1,0:T(8,128)(2,1)S(1)}, u32[]{:S(2)}, u32[]{:S(2)}) collective-permute-start(bf16[16,1024]{1,0:T(8,128)(2,1)S(1)} %get-tuple-element.26), channel_id=1, source_target_pairs={{0,2},{1,3},{2,4},{3,5},{4,6},{5,7},{8,10},{9,11},{10,12},{11,13},... | collective-permute-start | bytes 98312 | tf_op jit(solution)/shard_map/ppermute | solution.py:14
  241.7 3.8 %collective-permute-done.31 = bf16[16,1024]{1,0:T(8,128)(2,1)S(1)} collective-permute-done((bf16[16,1024]{1,0:T(8,128)(2,1)S(1)}, bf16[16,1024]{1,0:T(8,128)(2,1)S(1)}, u32[]{:S(2)}, u32[]{:S(2)}) %collective-permute-start.31) | collective-permute-done | bytes 32800 | tf_op jit(solution)/shard_map/ppermute | solution.py:14
  245.9 11.7 %all-gather.31.cloned.1.call-done = bf16[1,1024,1024]{2,1,0:T(8,128)(2,1)} async-done(((bf16[1,128,1024]{2,1,0:T(8,128)(2,1)}), bf16[1,1024,1024]{2,1,0:T(8,128)(2,1)}) %all-gather.31.cloned.1.call-update) | async-done | bytes 2097168 | tf_op jit(solution)/shard_map/all_gather | solution.py:67
  257.6 2.2 fusion.128
  260.3 27.8 %all_to_all.5 = bf16[2,4,128,1024]{3,2,0,1:T(8,128)(2,1)S(1)} all-to-all(bf16[2,4,128,1024]{3,2,0,1:T(8,128)(2,1)S(1)} %copy.10), channel_id=1, replica_groups=mesh['segment'=4,'graph'=8] {'segment'}, dimensions={1} | all-to-all | bytes 4194304 | tf_op jit(solution)/shard_map/all_to_all | solution.py:86
  288.0 1.5 copy.11
  (166 shorter events, 49.4 us)
Async XLA Ops:
  6.5 7.8 %copy-start = (bf16[512,1024]{1,0:T(8,128)(2,1)S(1)}, bf16[512,1024]{1,0:T(8,128)(2,1)}, u32[]{:S(2)}) copy-start(bf16[512,1024]{1,0:T(8,128)(2,1)} %param.12) | copy-start | bytes 3145732
  6.5 34.4 %all-gather.17.cloned.1.call-start = ((), (), s32[]{:S(2)}) async-start(), calls=%async_computation.1 | async-start | bytes 2359296 | tf_op jit(solution)/shard_map/all_gather | solution.py:67
  9.5 62.6 %all-gather.19.cloned.1.call-start = ((), (), s32[]{:S(2)}) async-start(), calls=%async_computation.2 | async-start | bytes 2359296 | tf_op jit(solution)/shard_map/all_gather | solution.py:67
  10.2 92.7 %all-gather.21.cloned.1.call-start = ((), (), s32[]{:S(2)}) async-start(), calls=%async_computation.3 | async-start | bytes 2359296 | tf_op jit(solution)/shard_map/all_gather | solution.py:67
  11.0 123.4 %all-gather.23.cloned.1.call-start = ((), (), s32[]{:S(2)}) async-start(), calls=%async_computation.4 | async-start | bytes 2359296 | tf_op jit(solution)/shard_map/all_gather | solution.py:67
  11.5 153.6 %all-gather.25.cloned.1.call-start = ((), (), s32[]{:S(2)}) async-start(), calls=%async_computation.5 | async-start | bytes 2359296 | tf_op jit(solution)/shard_map/all_gather | solution.py:67
  12.1 183.7 %all-gather.27.cloned.1.call-start = ((), (), s32[]{:S(2)}) async-start(), calls=%async_computation.6 | async-start | bytes 2359296 | tf_op jit(solution)/shard_map/all_gather | solution.py:67
  12.7 214.3 %all-gather.29.cloned.1.call-start = ((), (), s32[]{:S(2)}) async-start(), calls=%async_computation.7 | async-start | bytes 2359296 | tf_op jit(solution)/shard_map/all_gather | solution.py:67
  13.5 244.1 %all-gather.31.cloned.1.call-start = ((), (), s32[]{:S(2)}) async-start(), calls=%async_computation.8 | async-start | bytes 2359296 | tf_op jit(solution)/shard_map/all_gather | solution.py:67
  14.3 14.0 %copy-start.2 = (bf16[4,128,128]{2,1,0:T(8,128)(2,1)S(1)}, bf16[4,128,128]{2,1,0:T(8,128)(2,1)}, u32[]{:S(2)}) copy-start(bf16[4,128,128]{2,1,0:T(8,128)(2,1)} %param.15) | copy-start | bytes 393220
  15.8 21.8 %collective-permute-start = (bf16[16,1024]{1,0:T(8,128)(2,1)}, bf16[16,1024]{1,0:T(8,128)(2,1)}, u32[]{:S(2)}, u32[]{:S(2)}) collective-permute-start(bf16[16,1024]{1,0:T(8,128)(2,1)} %get-tuple-element.56), channel_id=1, source_target_pairs={{0,1},{1,2},{2,3},{3,4},{4,5},{5,6},{6,7},{8,9},{9,10},{10,11},{11... | collective-permute-start | bytes 98312 | tf_op jit(solution)/shard_map/ppermute | solution.py:14
  18.1 20.2 %collective-permute-start.1 = (bf16[16,1024]{1,0:T(8,128)(2,1)}, bf16[16,1024]{1,0:T(8,128)(2,1)S(1)}, u32[]{:S(2)}, u32[]{:S(2)}) collective-permute-start(bf16[16,1024]{1,0:T(8,128)(2,1)} %get-tuple-element.55), channel_id=1, source_target_pairs={{1,0},{2,1},{3,2},{4,3},{5,4},{6,5},{7,6},{9,8},{10,9},{11,10},{12... | collective-permute-start | bytes 98312 | tf_op jit(solution)/shard_map/ppermute | solution.py:14
  19.4 19.0 %collective-permute-start.2 = (bf16[16,1024]{1,0:T(8,128)(2,1)}, bf16[16,1024]{1,0:T(8,128)(2,1)S(1)}, u32[]{:S(2)}, u32[]{:S(2)}) collective-permute-start(bf16[16,1024]{1,0:T(8,128)(2,1)} %get-tuple-element.54), channel_id=1, source_target_pairs={{0,2},{1,3},{2,4},{3,5},{4,6},{5,7},{8,10},{9,11},{10,12},{11,13},... | collective-permute-start | bytes 98312 | tf_op jit(solution)/shard_map/ppermute | solution.py:14
  24.9 13.5 %collective-permute-start.3 = (bf16[16,1024]{1,0:T(8,128)(2,1)}, bf16[16,1024]{1,0:T(8,128)(2,1)S(1)}, u32[]{:S(2)}, u32[]{:S(2)}) collective-permute-start(bf16[16,1024]{1,0:T(8,128)(2,1)} %get-tuple-element.53), channel_id=1, source_target_pairs={{2,0},{3,1},{4,2},{5,3},{6,4},{7,5},{10,8},{11,9},{12,10},{13,11},... | collective-permute-start | bytes 98312 | tf_op jit(solution)/shard_map/ppermute | solution.py:14
  34.2 4.3 %copy-start.5 = (bf16[64,1024]{1,0:T(8,128)(2,1)S(1)}, bf16[64,1024]{1,0:T(8,128)(2,1)}, u32[]{:S(2)}) copy-start(bf16[64,1024]{1,0:T(8,128)(2,1)} %gather_fusion.1) | copy-start | bytes 393220
  43.9 10.5 %collective-permute-start.4 = (bf16[16,1024]{1,0:T(8,128)(2,1)S(1)}, bf16[16,1024]{1,0:T(8,128)(2,1)S(1)}, u32[]{:S(2)}, u32[]{:S(2)}) collective-permute-start(bf16[16,1024]{1,0:T(8,128)(2,1)S(1)} %get-tuple-element.52), channel_id=1, source_target_pairs={{0,1},{1,2},{2,3},{3,4},{4,5},{5,6},{6,7},{8,9},{9,10},{10,11},{11... | collective-permute-start | bytes 98312 | tf_op jit(solution)/shard_map/ppermute | solution.py:14
  46.2 8.1 %collective-permute-start.5 = (bf16[16,1024]{1,0:T(8,128)(2,1)S(1)}, bf16[16,1024]{1,0:T(8,128)(2,1)S(1)}, u32[]{:S(2)}, u32[]{:S(2)}) collective-permute-start(bf16[16,1024]{1,0:T(8,128)(2,1)S(1)} %get-tuple-element.51), channel_id=1, source_target_pairs={{1,0},{2,1},{3,2},{4,3},{5,4},{6,5},{7,6},{9,8},{10,9},{11,10},{12... | collective-permute-start | bytes 98312 | tf_op jit(solution)/shard_map/ppermute | solution.py:14
  47.5 7.6 %collective-permute-start.6 = (bf16[16,1024]{1,0:T(8,128)(2,1)S(1)}, bf16[16,1024]{1,0:T(8,128)(2,1)S(1)}, u32[]{:S(2)}, u32[]{:S(2)}) collective-permute-start(bf16[16,1024]{1,0:T(8,128)(2,1)S(1)} %get-tuple-element.50), channel_id=1, source_target_pairs={{0,2},{1,3},{2,4},{3,5},{4,6},{5,7},{8,10},{9,11},{10,12},{11,13},... | collective-permute-start | bytes 98312 | tf_op jit(solution)/shard_map/ppermute | solution.py:14
  53.0 7.1 %collective-permute-start.7 = (bf16[16,1024]{1,0:T(8,128)(2,1)S(1)}, bf16[16,1024]{1,0:T(8,128)(2,1)S(1)}, u32[]{:S(2)}, u32[]{:S(2)}) collective-permute-start(bf16[16,1024]{1,0:T(8,128)(2,1)S(1)} %get-tuple-element.49), channel_id=1, source_target_pairs={{2,0},{3,1},{4,2},{5,3},{6,4},{7,5},{10,8},{11,9},{12,10},{13,11},... | collective-permute-start | bytes 98312 | tf_op jit(solution)/shard_map/ppermute | solution.py:14
  74.9 10.3 %collective-permute-start.8 = (bf16[16,1024]{1,0:T(8,128)(2,1)S(1)}, bf16[16,1024]{1,0:T(8,128)(2,1)S(1)}, u32[]{:S(2)}, u32[]{:S(2)}) collective-permute-start(bf16[16,1024]{1,0:T(8,128)(2,1)S(1)} %get-tuple-element.48), channel_id=1, source_target_pairs={{0,1},{1,2},{2,3},{3,4},{4,5},{5,6},{6,7},{8,9},{9,10},{10,11},{11... | collective-permute-start | bytes 98312 | tf_op jit(solution)/shard_map/ppermute | solution.py:14
  77.3 8.0 %collective-permute-start.9 = (bf16[16,1024]{1,0:T(8,128)(2,1)S(1)}, bf16[16,1024]{1,0:T(8,128)(2,1)S(1)}, u32[]{:S(2)}, u32[]{:S(2)}) collective-permute-start(bf16[16,1024]{1,0:T(8,128)(2,1)S(1)} %get-tuple-element.47), channel_id=1, source_target_pairs={{1,0},{2,1},{3,2},{4,3},{5,4},{6,5},{7,6},{9,8},{10,9},{11,10},{12... | collective-permute-start | bytes 98312 | tf_op jit(solution)/shard_map/ppermute | solution.py:14
  78.6 7.5 %collective-permute-start.10 = (bf16[16,1024]{1,0:T(8,128)(2,1)S(1)}, bf16[16,1024]{1,0:T(8,128)(2,1)S(1)}, u32[]{:S(2)}, u32[]{:S(2)}) collective-permute-start(bf16[16,1024]{1,0:T(8,128)(2,1)S(1)} %get-tuple-element.46), channel_id=1, source_target_pairs={{0,2},{1,3},{2,4},{3,5},{4,6},{5,7},{8,10},{9,11},{10,12},{11,13},... | collective-permute-start | bytes 98312 | tf_op jit(solution)/shard_map/ppermute | solution.py:14
  84.0 7.3 %collective-permute-start.11 = (bf16[16,1024]{1,0:T(8,128)(2,1)S(1)}, bf16[16,1024]{1,0:T(8,128)(2,1)S(1)}, u32[]{:S(2)}, u32[]{:S(2)}) collective-permute-start(bf16[16,1024]{1,0:T(8,128)(2,1)S(1)} %get-tuple-element.45), channel_id=1, source_target_pairs={{2,0},{3,1},{4,2},{5,3},{6,4},{7,5},{10,8},{11,9},{12,10},{13,11},... | collective-permute-start | bytes 98312 | tf_op jit(solution)/shard_map/ppermute | solution.py:14
  105.9 10.4 %collective-permute-start.12 = (bf16[16,1024]{1,0:T(8,128)(2,1)S(1)}, bf16[16,1024]{1,0:T(8,128)(2,1)S(1)}, u32[]{:S(2)}, u32[]{:S(2)}) collective-permute-start(bf16[16,1024]{1,0:T(8,128)(2,1)S(1)} %get-tuple-element.44), channel_id=1, source_target_pairs={{0,1},{1,2},{2,3},{3,4},{4,5},{5,6},{6,7},{8,9},{9,10},{10,11},{11... | collective-permute-start | bytes 98312 | tf_op jit(solution)/shard_map/ppermute | solution.py:14
  108.2 8.0 %collective-permute-start.13 = (bf16[16,1024]{1,0:T(8,128)(2,1)S(1)}, bf16[16,1024]{1,0:T(8,128)(2,1)S(1)}, u32[]{:S(2)}, u32[]{:S(2)}) collective-permute-start(bf16[16,1024]{1,0:T(8,128)(2,1)S(1)} %get-tuple-element.43), channel_id=1, source_target_pairs={{1,0},{2,1},{3,2},{4,3},{5,4},{6,5},{7,6},{9,8},{10,9},{11,10},{12... | collective-permute-start | bytes 98312 | tf_op jit(solution)/shard_map/ppermute | solution.py:14
  109.5 7.5 %collective-permute-start.14 = (bf16[16,1024]{1,0:T(8,128)(2,1)S(1)}, bf16[16,1024]{1,0:T(8,128)(2,1)S(1)}, u32[]{:S(2)}, u32[]{:S(2)}) collective-permute-start(bf16[16,1024]{1,0:T(8,128)(2,1)S(1)} %get-tuple-element.42), channel_id=1, source_target_pairs={{0,2},{1,3},{2,4},{3,5},{4,6},{5,7},{8,10},{9,11},{10,12},{11,13},... | collective-permute-start | bytes 98312 | tf_op jit(solution)/shard_map/ppermute | solution.py:14
  114.9 7.2 %collective-permute-start.15 = (bf16[16,1024]{1,0:T(8,128)(2,1)S(1)}, bf16[16,1024]{1,0:T(8,128)(2,1)S(1)}, u32[]{:S(2)}, u32[]{:S(2)}) collective-permute-start(bf16[16,1024]{1,0:T(8,128)(2,1)S(1)} %get-tuple-element.41), channel_id=1, source_target_pairs={{2,0},{3,1},{4,2},{5,3},{6,4},{7,5},{10,8},{11,9},{12,10},{13,11},... | collective-permute-start | bytes 98312 | tf_op jit(solution)/shard_map/ppermute | solution.py:14
  137.2 9.8 %collective-permute-start.16 = (bf16[16,1024]{1,0:T(8,128)(2,1)S(1)}, bf16[16,1024]{1,0:T(8,128)(2,1)S(1)}, u32[]{:S(2)}, u32[]{:S(2)}) collective-permute-start(bf16[16,1024]{1,0:T(8,128)(2,1)S(1)} %get-tuple-element.40), channel_id=1, source_target_pairs={{0,1},{1,2},{2,3},{3,4},{4,5},{5,6},{6,7},{8,9},{9,10},{10,11},{11... | collective-permute-start | bytes 98312 | tf_op jit(solution)/shard_map/ppermute | solution.py:14
  139.6 7.4 %collective-permute-start.17 = (bf16[16,1024]{1,0:T(8,128)(2,1)S(1)}, bf16[16,1024]{1,0:T(8,128)(2,1)S(1)}, u32[]{:S(2)}, u32[]{:S(2)}) collective-permute-start(bf16[16,1024]{1,0:T(8,128)(2,1)S(1)} %get-tuple-element.39), channel_id=1, source_target_pairs={{1,0},{2,1},{3,2},{4,3},{5,4},{6,5},{7,6},{9,8},{10,9},{11,10},{12... | collective-permute-start | bytes 98312 | tf_op jit(solution)/shard_map/ppermute | solution.py:14
  140.9 6.9 %collective-permute-start.18 = (bf16[16,1024]{1,0:T(8,128)(2,1)S(1)}, bf16[16,1024]{1,0:T(8,128)(2,1)S(1)}, u32[]{:S(2)}, u32[]{:S(2)}) collective-permute-start(bf16[16,1024]{1,0:T(8,128)(2,1)S(1)} %get-tuple-element.38), channel_id=1, source_target_pairs={{0,2},{1,3},{2,4},{3,5},{4,6},{5,7},{8,10},{9,11},{10,12},{11,13},... | collective-permute-start | bytes 98312 | tf_op jit(solution)/shard_map/ppermute | solution.py:14
  145.7 7.2 %collective-permute-start.19 = (bf16[16,1024]{1,0:T(8,128)(2,1)S(1)}, bf16[16,1024]{1,0:T(8,128)(2,1)S(1)}, u32[]{:S(2)}, u32[]{:S(2)}) collective-permute-start(bf16[16,1024]{1,0:T(8,128)(2,1)S(1)} %get-tuple-element.37), channel_id=1, source_target_pairs={{2,0},{3,1},{4,2},{5,3},{6,4},{7,5},{10,8},{11,9},{12,10},{13,11},... | collective-permute-start | bytes 98312 | tf_op jit(solution)/shard_map/ppermute | solution.py:14
  168.0 9.8 %collective-permute-start.20 = (bf16[16,1024]{1,0:T(8,128)(2,1)S(1)}, bf16[16,1024]{1,0:T(8,128)(2,1)S(1)}, u32[]{:S(2)}, u32[]{:S(2)}) collective-permute-start(bf16[16,1024]{1,0:T(8,128)(2,1)S(1)} %get-tuple-element.36), channel_id=1, source_target_pairs={{0,1},{1,2},{2,3},{3,4},{4,5},{5,6},{6,7},{8,9},{9,10},{10,11},{11... | collective-permute-start | bytes 98312 | tf_op jit(solution)/shard_map/ppermute | solution.py:14
  170.4 7.4 %collective-permute-start.21 = (bf16[16,1024]{1,0:T(8,128)(2,1)S(1)}, bf16[16,1024]{1,0:T(8,128)(2,1)S(1)}, u32[]{:S(2)}, u32[]{:S(2)}) collective-permute-start(bf16[16,1024]{1,0:T(8,128)(2,1)S(1)} %get-tuple-element.35), channel_id=1, source_target_pairs={{1,0},{2,1},{3,2},{4,3},{5,4},{6,5},{7,6},{9,8},{10,9},{11,10},{12... | collective-permute-start | bytes 98312 | tf_op jit(solution)/shard_map/ppermute | solution.py:14
  171.7 6.9 %collective-permute-start.22 = (bf16[16,1024]{1,0:T(8,128)(2,1)S(1)}, bf16[16,1024]{1,0:T(8,128)(2,1)S(1)}, u32[]{:S(2)}, u32[]{:S(2)}) collective-permute-start(bf16[16,1024]{1,0:T(8,128)(2,1)S(1)} %get-tuple-element.34), channel_id=1, source_target_pairs={{0,2},{1,3},{2,4},{3,5},{4,6},{5,7},{8,10},{9,11},{10,12},{11,13},... | collective-permute-start | bytes 98312 | tf_op jit(solution)/shard_map/ppermute | solution.py:14
  176.5 7.2 %collective-permute-start.23 = (bf16[16,1024]{1,0:T(8,128)(2,1)S(1)}, bf16[16,1024]{1,0:T(8,128)(2,1)S(1)}, u32[]{:S(2)}, u32[]{:S(2)}) collective-permute-start(bf16[16,1024]{1,0:T(8,128)(2,1)S(1)} %get-tuple-element.33), channel_id=1, source_target_pairs={{2,0},{3,1},{4,2},{5,3},{6,4},{7,5},{10,8},{11,9},{12,10},{13,11},... | collective-permute-start | bytes 98312 | tf_op jit(solution)/shard_map/ppermute | solution.py:14
  197.9 17.3 %copy-start.4 = (bf16[64,1024]{1,0:T(8,128)(2,1)S(1)}, bf16[64,1024]{1,0:T(8,128)(2,1)}, u32[]{:S(2)}) copy-start(bf16[64,1024]{1,0:T(8,128)(2,1)} %gather_fusion.13) | copy-start | bytes 393220
  198.8 10.6 %collective-permute-start.24 = (bf16[16,1024]{1,0:T(8,128)(2,1)S(1)}, bf16[16,1024]{1,0:T(8,128)(2,1)S(1)}, u32[]{:S(2)}, u32[]{:S(2)}) collective-permute-start(bf16[16,1024]{1,0:T(8,128)(2,1)S(1)} %get-tuple-element.32), channel_id=1, source_target_pairs={{0,1},{1,2},{2,3},{3,4},{4,5},{5,6},{6,7},{8,9},{9,10},{10,11},{11... | collective-permute-start | bytes 98312 | tf_op jit(solution)/shard_map/ppermute | solution.py:14
  201.9 7.5 %collective-permute-start.25 = (bf16[16,1024]{1,0:T(8,128)(2,1)S(1)}, bf16[16,1024]{1,0:T(8,128)(2,1)S(1)}, u32[]{:S(2)}, u32[]{:S(2)}) collective-permute-start(bf16[16,1024]{1,0:T(8,128)(2,1)S(1)} %get-tuple-element.31), channel_id=1, source_target_pairs={{1,0},{2,1},{3,2},{4,3},{5,4},{6,5},{7,6},{9,8},{10,9},{11,10},{12... | collective-permute-start | bytes 98312 | tf_op jit(solution)/shard_map/ppermute | solution.py:14
  203.2 6.9 %collective-permute-start.26 = (bf16[16,1024]{1,0:T(8,128)(2,1)S(1)}, bf16[16,1024]{1,0:T(8,128)(2,1)S(1)}, u32[]{:S(2)}, u32[]{:S(2)}) collective-permute-start(bf16[16,1024]{1,0:T(8,128)(2,1)S(1)} %get-tuple-element.30), channel_id=1, source_target_pairs={{0,2},{1,3},{2,4},{3,5},{4,6},{5,7},{8,10},{9,11},{10,12},{11,13},... | collective-permute-start | bytes 98312 | tf_op jit(solution)/shard_map/ppermute | solution.py:14
  208.0 7.2 %collective-permute-start.27 = (bf16[16,1024]{1,0:T(8,128)(2,1)S(1)}, bf16[16,1024]{1,0:T(8,128)(2,1)S(1)}, u32[]{:S(2)}, u32[]{:S(2)}) collective-permute-start(bf16[16,1024]{1,0:T(8,128)(2,1)S(1)} %get-tuple-element.29), channel_id=1, source_target_pairs={{2,0},{3,1},{4,2},{5,3},{6,4},{7,5},{10,8},{11,9},{12,10},{13,11},... | collective-permute-start | bytes 98312 | tf_op jit(solution)/shard_map/ppermute | solution.py:14
  230.1 15.5 %copy-start.3 = (bf16[64,1024]{1,0:T(8,128)(2,1)S(1)}, bf16[64,1024]{1,0:T(8,128)(2,1)}, u32[]{:S(2)}) copy-start(bf16[64,1024]{1,0:T(8,128)(2,1)} %gather_fusion.15) | copy-start | bytes 393220
  230.2 11.4 %collective-permute-start.28 = (bf16[16,1024]{1,0:T(8,128)(2,1)S(1)}, bf16[16,1024]{1,0:T(8,128)(2,1)S(1)}, u32[]{:S(2)}, u32[]{:S(2)}) collective-permute-start(bf16[16,1024]{1,0:T(8,128)(2,1)S(1)} %get-tuple-element.28), channel_id=1, source_target_pairs={{0,1},{1,2},{2,3},{3,4},{4,5},{5,6},{6,7},{8,9},{9,10},{10,11},{11... | collective-permute-start | bytes 98312 | tf_op jit(solution)/shard_map/ppermute | solution.py:14
  232.3 9.3 %collective-permute-start.29 = (bf16[16,1024]{1,0:T(8,128)(2,1)S(1)}, bf16[16,1024]{1,0:T(8,128)(2,1)S(1)}, u32[]{:S(2)}, u32[]{:S(2)}) collective-permute-start(bf16[16,1024]{1,0:T(8,128)(2,1)S(1)} %get-tuple-element.27), channel_id=1, source_target_pairs={{1,0},{2,1},{3,2},{4,3},{5,4},{6,5},{7,6},{9,8},{10,9},{11,10},{12... | collective-permute-start | bytes 98312 | tf_op jit(solution)/shard_map/ppermute | solution.py:14
  233.6 8.0 %collective-permute-start.30 = (bf16[16,1024]{1,0:T(8,128)(2,1)S(1)}, bf16[16,1024]{1,0:T(8,128)(2,1)S(1)}, u32[]{:S(2)}, u32[]{:S(2)}) collective-permute-start(bf16[16,1024]{1,0:T(8,128)(2,1)S(1)} %get-tuple-element.26), channel_id=1, source_target_pairs={{0,2},{1,3},{2,4},{3,5},{4,6},{5,7},{8,10},{9,11},{10,12},{11,13},... | collective-permute-start | bytes 98312 | tf_op jit(solution)/shard_map/ppermute | solution.py:14
  238.2 7.3 %collective-permute-start.31 = (bf16[16,1024]{1,0:T(8,128)(2,1)S(1)}, bf16[16,1024]{1,0:T(8,128)(2,1)S(1)}, u32[]{:S(2)}, u32[]{:S(2)}) collective-permute-start(bf16[16,1024]{1,0:T(8,128)(2,1)S(1)} %get-tuple-element.25), channel_id=1, source_target_pairs={{2,0},{3,1},{4,2},{5,3},{6,4},{7,5},{10,8},{11,9},{12,10},{13,11},... | collective-permute-start | bytes 98312 | tf_op jit(solution)/shard_map/ppermute | solution.py:14
  257.6 2.3 copy-start.1
Sparse Core Ops, SparseCore 0:
  9.6 31.3 all-gather.16
  42.6 29.4 all-gather.18
  73.6 29.2 all-gather.20
  104.4 29.8 all-gather.22
  135.8 29.3 all-gather.24
  166.6 29.2 all-gather.26
  197.5 29.5 all-gather.28
  228.6 28.8 all-gather.30
where the time goes:
time: 301 us; the launch traced here: 296 us
  waiting for transfers between devices  126 us (42%)
  starting transfers between devices  79 us (26%)
  blocking collectives  27.8 us (9%)
  local copies, waits for them, and re-layouts  23.1 us (8%)
  matrix products  23 us (8%)
  between operations  14.4 us (5%)
  other arithmetic  3.52 us (1%)
    all_gather x8, waiting for transfers between devices, shards(): weight = lax.all_gather(weights[number], 'graph', axis=0, tiled=True)  82.8 us
    ppermute x32, starting transfers between devices, shifted(): lax.ppermute(value, axis, [(source, source + steps) for source in range(i...  78.7 us
    ppermute x32, waiting for transfers between devices, shifted(): lax.ppermute(value, axis, [(source, source + steps) for source in range(i...  39.1 us
    all_to_all x1, blocking collectives, shards(): lax.all_to_all(arranged, 'segment', split_axis=1, concat_axis=1, tiled=True)  27.8 us
    dot_general x8, matrix products, propagate(): jnp.dot(support.astype(jnp.bfloat16), weight, preferred_element_type=jnp....  16.9 us
    gather x8, local copies, waits for them, and re-layouts, propagate(): arrived.append(jnp.take(layer_table, past_rows, axis=0))  7.62 us
  transfers between devices with their start and end apart: 40, of which 21 were waited for; matrix products, arithmetic and copies ran while one was open for 14% of the time, Pallas kernels for 0%

commit v1 on v0

--- a/solution.py
+++ b/solution.py
@@ -1,6 +1,10 @@
+import math
+
 import jax
 import jax.numpy as jnp
 from jax import lax
+from jax.experimental import pallas as pl
+from jax.experimental.pallas import tpu as pltpu
 from jax.sharding import PartitionSpec as P
 
 ALPHA = 0.1
@@ -87,6 +91,368 @@
     return received.reshape(kept_slots, batch_count * batch_rows, features.shape[1])
 
 
+TILE_ROWS = 16
+MESH = pl.DeviceIdType.MESH
+
+
+def column_of(row):
+    count = row.shape[1]
+    down = lax.broadcasted_iota(jnp.int32, (count, count), 0)
+    across = lax.broadcasted_iota(jnp.int32, (count, count), 1)
+    spread = jnp.broadcast_to(row.astype(jnp.float32), (count, count))
+    return jnp.sum(jnp.where(down == across, spread, 0.0), axis=1, keepdims=True)
+
+
+def selector(row, width):
+    across = lax.broadcasted_iota(jnp.int32, (row.shape[1], width), 1).astype(jnp.float32)
+    return jnp.where(across == column_of(row), 1.0, 0.0).astype(jnp.bfloat16)
+
+
+def transposed_dot(left, right):
+    return lax.dot_general(
+        left, right, (((0,), (0,)), ((), ())), preferred_element_type=jnp.float32
+    )
+
+
+def stage_kernel(
+    segments, places, layer_total,
+    features, weights, history, own_adj, side_adj, hist_adj, send_ids, hist_ids,
+    out,
+    full, base, select, entering, leaving, arrived,
+    own_sem, full_recv, up_send, down_send, pair_send,
+    edge_send, edge_recv, hop_send, hop_recv,
+):
+    seg = lax.axis_index("segment")
+    me = lax.axis_index("graph")
+    kept = layer_total // segments
+    batches, rows = own_adj.shape[0], own_adj.shape[2]
+    shard = weights.shape[1]
+    edge = send_ids.shape[2]
+    chips = places // 2
+    chip = me // 2
+    core = me % 2
+    pair = me + 1 - 2 * core
+    first_layer = seg * kept
+
+    barrier = pltpu.get_barrier_semaphore()
+    expected = jnp.int32(0)
+    for offset in OFFSETS:
+        there = me + offset
+        inside = jnp.logical_and(there >= 0, there < places)
+
+        @pl.when(inside)
+        def _():
+            pl.semaphore_signal(barrier, inc=1, device_id={"graph": there}, device_id_type=MESH)
+
+        expected = expected + inside.astype(jnp.int32)
+    for step in (1, -1):
+        beside = seg + step
+        inside = jnp.logical_and(beside >= 0, beside < segments)
+
+        @pl.when(inside)
+        def _():
+            pl.semaphore_signal(
+                barrier, inc=1, device_id={"segment": beside}, device_id_type=MESH
+            )
+
+        expected = expected + inside.astype(jnp.int32)
+    pl.semaphore_wait(barrier, expected)
+
+    def block(slot, owner):
+        return full.at[slot, pl.ds(pl.multiple_of(owner * shard, shard), shard)]
+
+    def push(slot, owner, source, target, send_sem):
+        return pltpu.make_async_remote_copy(
+            src_ref=source,
+            dst_ref=block(slot, owner),
+            send_sem=send_sem.at[slot, owner // 2],
+            recv_sem=full_recv.at[slot, owner],
+            device_id={"graph": target},
+            device_id_type=MESH,
+        )
+
+    def landed(slot, owner):
+        push(slot, owner, block(slot, owner), pair, pair_send).wait_recv()
+
+    def own_copy(slot):
+        return pltpu.make_async_copy(
+            weights.at[first_layer + slot], block(slot, me), own_sem.at[slot]
+        )
+
+    def open_slot(slot):
+        source = weights.at[first_layer + slot]
+
+        @pl.when(chip < chips - 1)
+        def _():
+            push(slot, me, source, me + 2, up_send).start()
+
+        @pl.when(chip > 0)
+        def _():
+            push(slot, me, source, me - 2, down_send).start()
+
+        push(slot, me, source, pair, pair_send).start()
+        own_copy(slot).start()
+
+    def relay(slot, distance):
+        below = me - 2 * distance
+
+        @pl.when(below >= 0)
+        def _():
+            landed(slot, below)
+
+            @pl.when(chip < chips - 1)
+            def _():
+                push(slot, below, block(slot, below), me + 2, up_send).start()
+
+            push(slot, below, block(slot, below), pair, pair_send).start()
+
+        above = me + 2 * distance
+
+        @pl.when(above < places)
+        def _():
+            landed(slot, above)
+
+            @pl.when(chip > 0)
+            def _():
+                push(slot, above, block(slot, above), me - 2, down_send).start()
+
+            push(slot, above, block(slot, above), pair, pair_send).start()
+
+    def close_slot(slot):
+        own_copy(slot).wait()
+
+        def from_pair(other, carry):
+            landed(slot, 2 * other + 1 - core)
+            return carry
+
+        lax.fori_loop(0, chips, from_pair, 0)
+
+    def edge_copy(slot, batch, direction):
+        part = pl.ds(direction * edge, edge)
+        return pltpu.make_async_remote_copy(
+            src_ref=leaving.at[slot, batch, part],
+            dst_ref=arrived.at[slot, batch, part],
+            send_sem=edge_send.at[slot, batch, direction],
+            recv_sem=edge_recv.at[slot, batch, direction],
+            device_id={"graph": me + OFFSETS[direction]},
+            device_id_type=MESH,
+        )
+
+    def sends(direction):
+        there = me + OFFSETS[direction]
+        return jnp.logical_and(there >= 0, there < places)
+
+    def receives(direction):
+        there = me - OFFSETS[direction]
+        return jnp.logical_and(there >= 0, there < places)
+
+    def send_edges(slot, batch, current):
+        leaving[slot, batch] = jnp.dot(
+            select[batch], current, preferred_element_type=jnp.float32
+        ).astype(jnp.bfloat16)
+        for direction in range(len(OFFSETS)):
+
+            @pl.when(sends(direction))
+            def _():
+                edge_copy(slot, batch, direction).start()
+
+    def batch_range(batch):
+        return pl.ds(pl.multiple_of(batch * rows, rows), rows)
+
+    def hop(batch):
+        return pltpu.make_async_remote_copy(
+            src_ref=out.at[kept - 1, batch_range(batch)],
+            dst_ref=entering.at[batch],
+            send_sem=hop_send.at[batch],
+            recv_sem=hop_recv.at[batch],
+            device_id={"segment": seg + 1},
+            device_id_type=MESH,
+        )
+
+    def prepare(batch, carry):
+        for direction in range(len(OFFSETS)):
+            part = pl.ds(direction * edge, edge)
+            select[batch, part] = selector(
+                send_ids[batch, pl.ds(direction, 1), :], rows
+            )
+            for slot in range(kept):
+
+                @pl.when(jnp.logical_not(receives(direction)))
+                def _():
+                    arrived[slot, batch, part] = jnp.zeros(
+                        (edge, arrived.shape[3]), jnp.bfloat16
+                    )
+
+        initial = features[batch_range(batch), :]
+
+        @pl.when(seg == 0)
+        def _():
+            entering[batch] = initial
+
+        lookup = selector(hist_ids[pl.ds(batch, 1), :], history.shape[1])
+        for slot in range(kept):
+            looked = jnp.dot(
+                lookup, history[first_layer + slot], preferred_element_type=jnp.float32
+            ).astype(jnp.bfloat16)
+            past = transposed_dot(hist_adj[batch], looked)
+            base[slot, batch] = (1.0 - ALPHA) * past + ALPHA * initial.astype(jnp.float32)
+        return carry
+
+    def layer(slot, batch):
+        strength = jnp.float32(0.0)
+        for number in range(layer_total):
+            value = math.log(LAMBDA / (number + 1.0) + 1.0)
+            strength = jnp.where(first_layer + slot == number, jnp.float32(value), strength)
+        if slot == 0:
+            current = entering[batch]
+        else:
+            current = out[slot - 1, batch_range(batch), :]
+        aggregate = jnp.dot(own_adj[batch], current, preferred_element_type=jnp.float32)
+        for direction in range(len(OFFSETS)):
+
+            @pl.when(receives(direction))
+            def _():
+                edge_copy(slot, batch, direction).wait_recv()
+
+        aggregate = aggregate + transposed_dot(side_adj[batch], arrived[slot, batch])
+        support = (1.0 - ALPHA) * aggregate + base[slot, batch]
+        mixing = jnp.dot(
+            support.astype(jnp.bfloat16), full[slot], preferred_element_type=jnp.float32
+        )
+        result = jnp.maximum((1.0 - strength) * support + strength * mixing, 0.0)
+        result = result.astype(jnp.bfloat16)
+        out[slot, batch_range(batch), :] = result
+        if slot < kept - 1:
+            send_edges(slot + 1, batch, result)
+        else:
+
+            @pl.when(seg < segments - 1)
+            def _():
+                hop(batch).start()
+
+    open_slot(0)
+    lax.fori_loop(0, batches, prepare, 0)
+    for slot in range(kept):
+        for distance in range(1, chips):
+            relay(slot, distance)
+            if slot < kept - 1 and distance == max(1, chips - 2):
+                open_slot(slot + 1)
+    for slot in range(kept):
+        close_slot(slot)
+
+    def tick(time, carry):
+        @pl.when(time < batches)
+        def _():
+            @pl.when(seg > 0)
+            def _():
+                hop(time).wait_recv()
+
+            send_edges(0, time, entering[time])
+
+        for slot in range(kept - 1, -1, -1):
+            batch = time - slot
+
+            @pl.when(jnp.logical_and(batch >= 0, batch < batches))
+            def _():
+                layer(slot, batch)
+
+        return carry
+
+    lax.fori_loop(0, batches + kept - 1, tick, 0)
+
+    def finish(batch, carry):
+        for slot in range(kept):
+            for direction in range(len(OFFSETS)):
+
+                @pl.when(sends(direction))
+                def _():
+                    edge_copy(slot, batch, direction).wait_send()
+
+        @pl.when(seg < segments - 1)
+        def _():
+            hop(batch).wait_send()
+
+        return carry
+
+    lax.fori_loop(0, batches, finish, 0)
+
+    def drain(other, carry):
+        owner = 2 * other + core
+        for slot in range(kept):
+            push(slot, owner, block(slot, owner), pair, pair_send).wait_send()
+
+            @pl.when(jnp.logical_and(other <= chip, chip < chips - 1))
+            def _():
+                push(slot, owner, block(slot, owner), me + 2, up_send).wait_send()
+
+            @pl.when(jnp.logical_and(other >= chip, chip > 0))
+            def _():
+                push(slot, owner, block(slot, owner), me - 2, down_send).wait_send()
+
+        return carry
+
+    lax.fori_loop(0, chips, drain, 0)
+
+
+def staged(features, weights, history, own_adj, side_adj, hist_adj, send_ids, hist_ids):
+    segments = lax.axis_size("segment")
+    places = lax.axis_size("graph")
+    layer_total, shard, width = weights.shape
+    kept = layer_total // segments
+    batches, rows = own_adj.shape[0], own_adj.shape[2]
+    edges = side_adj.shape[1] * side_adj.shape[2]
+    chips = places // 2
+    dma = pltpu.SemaphoreType.DMA
+
+    def kernel(*refs):
+        stage_kernel(segments, places, layer_total, *refs)
+
+    vmem = pl.BlockSpec(memory_space=pltpu.VMEM)
+    return pl.pallas_call(
+        kernel,
+        out_shape=jax.ShapeDtypeStruct((kept, batches * rows, width), jnp.bfloat16),
+        in_specs=[vmem, pl.BlockSpec(memory_space=pl.ANY)] + [vmem] * 6,
+        out_specs=vmem,
+        scratch_shapes=[
+            pltpu.VMEM((kept, places * shard, width), jnp.bfloat16),
+            pltpu.VMEM((kept, batches, rows, width), jnp.float32),
+            pltpu.VMEM((batches, edges, rows), jnp.bfloat16),
+            pltpu.VMEM((batches, rows, width), jnp.bfloat16),
+            pltpu.VMEM((kept, batches, edges, width), jnp.bfloat16),
+            pltpu.VMEM((kept, batches, edges, width), jnp.bfloat16),
+            dma((kept,)),
+            dma((kept, places)),
+            dma((kept, chips)),
+            dma((kept, chips)),
+            dma((kept, chips)),
+            dma((kept, batches, len(OFFSETS))),
+            dma((kept, batches, len(OFFSETS))),
+            dma((batches,)),
+            dma((batches,)),
+        ],
+        compiler_params=pltpu.CompilerParams(
+            collective_id=0, has_side_effects=True, vmem_limit_bytes=40 * 1024 * 1024
+        ),
+    )(
+        features,
+        weights,
+        history,
+        own_adj,
+        side_adj.reshape(batches, edges, rows),
+        hist_adj,
+        send_ids,
+        hist_ids,
+    )
+
+
+def device_part(features, weights, *rest):
+    places = lax.axis_size("graph")
+    whole_tiles = weights.shape[1] % TILE_ROWS == 0 and rest[2].shape[2] % TILE_ROWS == 0
+    if whole_tiles and places % 2 == 0 and weights.shape[0] % lax.axis_size("segment") == 0:
+        return staged(features, weights, *rest)
+    return shards(features, weights, *rest)
+
+
 def solution(mesh):
     in_specs = (
         P("graph", None),
@@ -99,4 +465,4 @@
         P(None, "graph"),
     )
     out_specs = P("segment", "graph", None)
-    return jax.shard_map(shards, mesh=mesh, in_specs=in_specs, out_specs=out_specs, check_vma=False)
+    return jax.shard_map(device_part, mesh=mesh, in_specs=in_specs, out_specs=out_specs, check_vma=False)

time: 301 us -> 124 us (0.41); the launches traced: 296 us -> 123 us
  waiting for transfers between devices: 126 us -> 0 us
  Pallas kernels: 0 us -> 114 us
  starting transfers between devices: 79 us -> 0 us
  blocking collectives: 27.8 us -> 0 us
  matrix products: 23 us -> 0 us
  between operations: 14.4 us -> 0.02 us
  local copies, waits for them, and re-layouts: 23.1 us -> 9.32 us
  other arithmetic: 3.52 us -> 0 us
    pallas_call x0 -> x1, Pallas kernels: none -> 114 us  [staged(): pl.pallas_call(kernel, out_shape=jax.ShapeDtypeStruct((kept, batches * ro...]
    all_gather x8 -> x0, waiting for transfers between devices: 82.8 us -> none  [shards(): weight = lax.all_gather(weights[number], 'graph', axis=0, tiled=True)]
    ppermute x32 -> x0, starting transfers between devices: 78.7 us -> none  [shifted(): lax.ppermute(value, axis, [(source, source + steps) for source in range(i...]
    ppermute x32 -> x0, waiting for transfers between devices: 39.1 us -> none  [shifted(): lax.ppermute(value, axis, [(source, source + steps) for source in range(i...]
    all_to_all x1 -> x0, blocking collectives: 27.8 us -> none  [shards(): lax.all_to_all(arranged, 'segment', split_axis=1, concat_axis=1, tiled=True)]
    dot_general x24 -> x0, matrix products: 23 us -> none  [the longest x8 16.9 us: propagate(): jnp.dot(support.astype(jnp.bfloat16), weight, preferred_element_type=jnp....]
    gather x16 -> x0, local copies, waits for them, and re-layouts: 13.3 us -> none  [the longest x8 7.62 us: propagate(): arrived.append(jnp.take(layer_table, past_rows, axis=0))]
    unnamed x44 -> x17, local copies, waits for them, and re-layouts: 0.91 us -> 9.32 us
  transfers between devices with their start and end apart: 40 -> 0, of which waited for: 21 -> 0; matrix products, arithmetic and copies ran while one was open for 14% -> 0% of each run, Pallas kernels for 0% -> 0%
where the time goes in v1:
time: 124 us; the launch traced here: 123 us
  Pallas kernels  114 us (92%)
  local copies, waits for them, and re-layouts  9.32 us (8%)
    pallas_call x1, Pallas kernels, staged(): pl.pallas_call(kernel, out_shape=jax.ShapeDtypeStruct((kept, batches * ro...  114 us
    unnamed x17, local copies, waits for them, and re-layouts  9.32 us

profile of v1, /device:TPU:6, one launch (start us, length us, event | category | flops | bytes accessed | tf_op | source)
XLA Modules:
  0.0 123.4 jit_solution(6706799394015219608)
XLA Ops:
  0.0 0.0 copy-start
  0.0 1.6 %copy-done = bf16[8,128,1024]{2,1,0:T(8,128)(2,1)S(1)} copy-done((bf16[8,128,1024]{2,1,0:T(8,128)(2,1)S(1)}, bf16[8,128,1024]{2,1,0:T(8,128)(2,1)}, u32[]{:S(2)}) %copy-start) | copy-done | bytes 2097176
  1.6 0.0 copy-start.1
  1.6 1.2 copy-done.1
  2.8 0.0 copy-start.2
  2.8 1.2 copy-done.2
  4.0 0.0 copy-start.3
  4.0 0.9 copy-done.3
  4.9 0.0 copy-start.4
  4.9 0.8 copy-done.4
  5.8 0.0 copy-start.5
  5.8 0.8 copy-done.5
  6.6 0.0 copy-start.6
  6.6 0.7 copy-done.6
  7.3 0.0 copy-start.7
  7.3 0.7 copy-done.7
  8.0 114.1 %shard_map.82 = bf16[2,512,1024]{2,1,0:T(8,128)(2,1)S(1)} custom-call(bf16[512,1024]{1,0:T(8,128)(2,1)S(1)} %copy-done.1, bf16[8,128,1024]{2,1,0:T(8,128)(2,1)S(1)} %copy-done, bf16[8,64,1024]{2,1,0:T(8,128)(2,1)S(1)} %copy-done.2, bf16[4,128,128]{2,1,0:T(8,128)(2,1)S(1)} %copy-done.3, bf16[4,64,128]{2,1,0:T(8,128)(2,1)S(1)} %bitcast.1, ...), custom_call_target="tpu_custom_call" | custom-call | tf_op jit(solution)/shard_map/pallas_call | solution.py:411
  122.1 1.3 %copy.10 = bf16[2,512,1024]{2,1,0:T(8,128)(2,1)} copy(bf16[2,512,1024]{2,1,0:T(8,128)(2,1)S(1)} %shard_map.82) | data formatting | bytes 4194304
Async XLA Ops:
  0.0 1.6 %copy-start = (bf16[8,128,1024]{2,1,0:T(8,128)(2,1)S(1)}, bf16[8,128,1024]{2,1,0:T(8,128)(2,1)}, u32[]{:S(2)}) copy-start(bf16[8,128,1024]{2,1,0:T(8,128)(2,1)} %refs_1_.1) | copy-start | bytes 6291460
  1.6 1.2 copy-start.1
  2.8 1.2 copy-start.2
  4.0 0.9 copy-start.3
  4.9 0.8 copy-start.4
  5.8 0.8 copy-start.5
  6.6 0.7 copy-start.6
  7.3 0.7 copy-start.7

commit v2 on v1

--- a/solution.py
+++ b/solution.py
@@ -116,10 +116,12 @@
 
 def stage_kernel(
     segments, places, layer_total,
-    features, weights, history, own_adj, side_adj, hist_adj, send_ids, hist_ids,
+    features_in, weights, history_in, own_in, side_in, hist_in, send_in, ids_in,
     out,
-    full, base, select, entering, leaving, arrived,
-    own_sem, full_recv, up_send, down_send, pair_send,
+    features, history, own_adj, side_adj, hist_adj, send_ids, hist_ids,
+    made, full, base, select, entering, leaving, arrived,
+    load_sem, own_sem, store_sem, line_recv, mate_recv, pair_recv, shard_recv,
+    up_send, down_send, mate_send, pair_send, shard_send,
     edge_send, edge_recv, hop_send, hop_recv,
 ):
     seg = lax.axis_index("segment")
@@ -127,15 +129,37 @@
     kept = layer_total // segments
     batches, rows = own_adj.shape[0], own_adj.shape[2]
     shard = weights.shape[1]
+    piece = shard // 2
     edge = send_ids.shape[2]
     chips = places // 2
     chip = me // 2
     core = me % 2
     pair = me + 1 - 2 * core
+    half = segments // 2
+    side = seg // half
+    mate = seg + half - 2 * half * side
     first_layer = seg * kept
 
+    loads = [
+        pltpu.make_async_copy(source, target, load_sem.at[number])
+        for number, (source, target) in enumerate(
+            [
+                (features_in, features),
+                (history_in.at[pl.ds(first_layer, kept)], history),
+                (own_in, own_adj),
+                (side_in, side_adj),
+                (hist_in, hist_adj),
+                (send_in, send_ids),
+                (ids_in, hist_ids),
+            ]
+        )
+    ]
+    for load in loads:
+        load.start()
+
     barrier = pltpu.get_barrier_semaphore()
-    expected = jnp.int32(0)
+    expected = jnp.int32(1)
+    pl.semaphore_signal(barrier, inc=1, device_id={"segment": mate}, device_id_type=MESH)
     for offset in OFFSETS:
         there = me + offset
         inside = jnp.logical_and(there >= 0, there < places)
@@ -158,71 +182,142 @@
         expected = expected + inside.astype(jnp.int32)
     pl.semaphore_wait(barrier, expected)
 
-    def block(slot, owner):
-        return full.at[slot, pl.ds(pl.multiple_of(owner * shard, shard), shard)]
-
-    def push(slot, owner, source, target, send_sem):
+
+    def shard_rows(owner):
+        return pl.ds(pl.multiple_of(owner * shard, shard), shard)
+
+    def piece_rows(owner, which):
+        return pl.ds(pl.multiple_of(owner * shard + which * piece, piece), piece)
+
+    def whole_shard(slot):
+        return weights.at[first_layer + slot]
+
+    def own_copy(slot):
+        return pltpu.make_async_copy(
+            whole_shard(slot), full.at[side, slot, shard_rows(me)], own_sem.at[slot]
+        )
+
+    def push(turn, slot, source, owner, which, target, send_sem, recv_sem):
         return pltpu.make_async_remote_copy(
             src_ref=source,
-            dst_ref=block(slot, owner),
-            send_sem=send_sem.at[slot, owner // 2],
-            recv_sem=full_recv.at[slot, owner],
-            device_id={"graph": target},
+            dst_ref=full.at[turn, slot, piece_rows(owner, which)],
+            send_sem=send_sem,
+            recv_sem=recv_sem,
+            device_id=target,
             device_id_type=MESH,
         )
 
-    def landed(slot, owner):
-        push(slot, owner, block(slot, owner), pair, pair_send).wait_recv()
-
-    def own_copy(slot):
-        return pltpu.make_async_copy(
-            weights.at[first_layer + slot], block(slot, me), own_sem.at[slot]
-        )
-
-    def open_slot(slot):
-        source = weights.at[first_layer + slot]
+    def held(turn, slot, owner, which):
+        return full.at[turn, slot, piece_rows(owner, which)]
+
+    def along(turn, slot, source, owner, step, send_sem):
+        return push(
+            turn, slot, source, owner, side, {"graph": me + 2 * step},
+            send_sem.at[turn, slot, owner // 2], line_recv.at[turn, slot, owner // 2],
+        )
+
+    def to_pair(slot, owner, which):
+        return push(
+            side, slot, held(side, slot, owner, which), owner, which, {"graph": pair},
+            pair_send.at[slot, which, owner // 2], pair_recv.at[slot, which, owner // 2],
+        )
+
+    def to_mate(slot, owner):
+        turn = 1 - side
+        return push(
+            turn, slot, held(turn, slot, owner, side), owner, side, {"segment": mate},
+            mate_send.at[slot, owner // 2], mate_recv.at[slot, owner // 2],
+        )
+
+    def from_mate(slot, owner):
+        which = 1 - side
+        return push(
+            side, slot, held(side, slot, owner, which), owner, which, {"segment": mate},
+            mate_send.at[slot, owner // 2], mate_recv.at[slot, owner // 2],
+        )
+
+    def shard_to_pair(slot, source, owner):
+        return pltpu.make_async_remote_copy(
+            src_ref=source,
+            dst_ref=full.at[side, slot, shard_rows(owner)],
+            send_sem=shard_send.at[slot],
+            recv_sem=shard_recv.at[slot],
+            device_id={"graph": pair},
+            device_id_type=MESH,
+        )
+
+    def open_slot(turn, slot):
+        number = (seg + (turn - side) * half) * kept + slot
+        source = weights.at[number, pl.ds(pl.multiple_of(side * piece, piece), piece)]
 
         @pl.when(chip < chips - 1)
         def _():
-            push(slot, me, source, me + 2, up_send).start()
+            along(turn, slot, source, me, 1, up_send).start()
 
         @pl.when(chip > 0)
         def _():
-            push(slot, me, source, me - 2, down_send).start()
-
-        push(slot, me, source, pair, pair_send).start()
-        own_copy(slot).start()
-
-    def relay(slot, distance):
+            along(turn, slot, source, me, -1, down_send).start()
+
+        @pl.when(side == turn)
+        def _():
+            shard_to_pair(slot, whole_shard(slot), me).start()
+            own_copy(slot).start()
+
+    def hand_on(turn, slot, owner):
+        @pl.when(side == turn)
+        def _():
+            to_pair(slot, owner, side).start()
+
+        @pl.when(side != turn)
+        def _():
+            to_mate(slot, owner).start()
+
+    def relay(turn, slot, distance):
         below = me - 2 * distance
 
         @pl.when(below >= 0)
         def _():
-            landed(slot, below)
+            block = held(turn, slot, below, side)
+            along(turn, slot, block, below, 1, up_send).wait_recv()
 
             @pl.when(chip < chips - 1)
             def _():
-                push(slot, below, block(slot, below), me + 2, up_send).start()
-
-            push(slot, below, block(slot, below), pair, pair_send).start()
+                along(turn, slot, block, below, 1, up_send).start()
+
+            hand_on(turn, slot, below)
 
         above = me + 2 * distance
 
         @pl.when(above < places)
         def _():
-            landed(slot, above)
+            block = held(turn, slot, above, side)
+            along(turn, slot, block, above, -1, down_send).wait_recv()
 
             @pl.when(chip > 0)
             def _():
-                push(slot, above, block(slot, above), me - 2, down_send).start()
-
-            push(slot, above, block(slot, above), pair, pair_send).start()
+                along(turn, slot, block, above, -1, down_send).start()
+
+            hand_on(turn, slot, above)
+
+    def bridge(slot, distance):
+        for owner in (me - 2 * distance, me + 2 * distance):
+
+            @pl.when(jnp.logical_and(owner >= 0, owner < places))
+            def _():
+                from_mate(slot, owner).wait_recv()
+                to_pair(slot, owner, 1 - side).start()
 
     def close_slot(slot):
         own_copy(slot).wait()
+        shard_to_pair(slot, full.at[side, slot, shard_rows(pair)], pair).wait_recv()
 
         def from_pair(other, carry):
-            landed(slot, 2 * other + 1 - core)
+            @pl.when(other != chip)
+            def _():
+                owner = 2 * other + 1 - core
+                for which in range(2):
+                    to_pair(slot, owner, which).wait_recv()
+
             return carry
 
         lax.fori_loop(0, chips, from_pair, 0)
@@ -259,9 +354,16 @@
     def batch_range(batch):
         return pl.ds(pl.multiple_of(batch * rows, rows), rows)
 
+    def store(slot, batch):
+        return pltpu.make_async_copy(
+            made.at[slot, batch_range(batch)],
+            out.at[slot, batch_range(batch)],
+            store_sem.at[slot, batch],
+        )
+
     def hop(batch):
         return pltpu.make_async_remote_copy(
-            src_ref=out.at[kept - 1, batch_range(batch)],
+            src_ref=made.at[kept - 1, batch_range(batch)],
             dst_ref=entering.at[batch],
             send_sem=hop_send.at[batch],
             recv_sem=hop_recv.at[batch],
@@ -292,7 +394,7 @@
         lookup = selector(hist_ids[pl.ds(batch, 1), :], history.shape[1])
         for slot in range(kept):
             looked = jnp.dot(
-                lookup, history[first_layer + slot], preferred_element_type=jnp.float32
+                lookup, history[slot], preferred_element_type=jnp.float32
             ).astype(jnp.bfloat16)
             past = transposed_dot(hist_adj[batch], looked)
             base[slot, batch] = (1.0 - ALPHA) * past + ALPHA * initial.astype(jnp.float32)
@@ -306,7 +408,7 @@
         if slot == 0:
             current = entering[batch]
         else:
-            current = out[slot - 1, batch_range(batch), :]
+            current = made[slot - 1, batch_range(batch), :]
         aggregate = jnp.dot(own_adj[batch], current, preferred_element_type=jnp.float32)
         for direction in range(len(OFFSETS)):
 
@@ -317,11 +419,12 @@
         aggregate = aggregate + transposed_dot(side_adj[batch], arrived[slot, batch])
         support = (1.0 - ALPHA) * aggregate + base[slot, batch]
         mixing = jnp.dot(
-            support.astype(jnp.bfloat16), full[slot], preferred_element_type=jnp.float32
+            support.astype(jnp.bfloat16), full[side, slot], preferred_element_type=jnp.float32
         )
         result = jnp.maximum((1.0 - strength) * support + strength * mixing, 0.0)
         result = result.astype(jnp.bfloat16)
-        out[slot, batch_range(batch), :] = result
+        made[slot, batch_range(batch), :] = result
+        store(slot, batch).start()
         if slot < kept - 1:
             send_edges(slot + 1, batch, result)
         else:
@@ -330,15 +433,78 @@
             def _():
                 hop(batch).start()
 
-    open_slot(0)
+    far = chips - 1
+
+    def line_steps(turn, slot):
+        steps = []
+        for distance in range(1, chips):
+            work = [(relay, (turn, slot, distance))]
+            if distance == max(1, far - 1):
+                if slot < kept - 1:
+                    work.append((open_slot, (turn, slot + 1)))
+                elif turn == 0:
+                    work.append((open_slot, (1, 0)))
+            steps.append(work)
+        return steps
+
+    def run(work):
+        for action, arguments in work:
+            action(*arguments)
+
+    def bridges(slot):
+        for distance in range(1, chips):
+            bridge(slot, distance)
+
+    open_slot(0, 0)
+    for load in loads:
+        load.wait()
     lax.fori_loop(0, batches, prepare, 0)
+    for work in line_steps(0, 0):
+        run(work)
+
+    @pl.when(side == 0)
+    def _():
+        bridges(0)
+
+    last_first = batches * kept - 1
+    last_other = batches + kept - 2
+    first_tasks = [[] for _ in range(last_first + 1)]
+    other_tasks = [[] for _ in range(last_other + 1)]
+    later = []
+    for slot in range(1, kept):
+        steps = line_steps(0, slot)
+        for distance in range(1, chips):
+            if distance > 1:
+                steps[distance - 1].append((bridge, (slot, distance - 1)))
+        steps.append([(bridge, (slot, far))])
+        for number, work in enumerate(steps):
+            first_tasks[min((slot - 1) * batches + number, slot * batches - 1)] += work
+        later += steps
+    shared = []
     for slot in range(kept):
-        for distance in range(1, chips):
-            relay(slot, distance)
-            if slot < kept - 1 and distance == max(1, chips - 2):
-                open_slot(slot + 1)
-    for slot in range(kept):
-        close_slot(slot)
+        shared += line_steps(1, slot)
+    for number, work in enumerate(shared):
+        first_tasks[min((kept - 1) * batches + number, last_first)] += work
+    for number, work in enumerate(shared[far:]):
+        other_tasks[min(number, last_other)] += work
+
+    @pl.when(jnp.logical_and(seg > 0, side == 0))
+    def _():
+        for work in later + shared[:far]:
+            run(work)
+
+    @pl.when(side == 1)
+    def _():
+        for slot in range(1, kept):
+            for work in line_steps(0, slot):
+                run(work)
+        for work in shared:
+            run(work)
+        for slot in range(kept):
+            bridges(slot)
+
+    lag = jnp.where(seg == 0, batches, 1)
+    ticks = batches + lag * (kept - 1)
 
     def tick(time, carry):
         @pl.when(time < batches)
@@ -349,19 +515,37 @@
 
             send_edges(0, time, entering[time])
 
+        for number, work in enumerate(first_tasks):
+
+            @pl.when(jnp.logical_and(seg == 0, time == number))
+            def _():
+                run(work)
+
         for slot in range(kept - 1, -1, -1):
-            batch = time - slot
+
+            @pl.when(time == lag * slot)
+            def _():
+                close_slot(slot)
+
+            batch = time - lag * slot
 
             @pl.when(jnp.logical_and(batch >= 0, batch < batches))
             def _():
                 layer(slot, batch)
 
+        for number, work in enumerate(other_tasks):
+
+            @pl.when(jnp.logical_and(jnp.logical_and(seg > 0, side == 0), time == number))
+            def _():
+                run(work)
+
         return carry
 
-    lax.fori_loop(0, batches + kept - 1, tick, 0)
+    lax.fori_loop(0, ticks, tick, 0)
 
     def finish(batch, carry):
         for slot in range(kept):
+            store(slot, batch).wait()
             for direction in range(len(OFFSETS)):
 
                 @pl.when(sends(direction))
@@ -379,15 +563,26 @@
     def drain(other, carry):
         owner = 2 * other + core
         for slot in range(kept):
-            push(slot, owner, block(slot, owner), pair, pair_send).wait_send()
-
-            @pl.when(jnp.logical_and(other <= chip, chip < chips - 1))
-            def _():
-                push(slot, owner, block(slot, owner), me + 2, up_send).wait_send()
-
-            @pl.when(jnp.logical_and(other >= chip, chip > 0))
-            def _():
-                push(slot, owner, block(slot, owner), me - 2, down_send).wait_send()
+            for turn in range(2):
+                block = held(turn, slot, owner, side)
+
+                @pl.when(jnp.logical_and(other <= chip, chip < chips - 1))
+                def _():
+                    along(turn, slot, block, owner, 1, up_send).wait_send()
+
+                @pl.when(jnp.logical_and(other >= chip, chip > 0))
+                def _():
+                    along(turn, slot, block, owner, -1, down_send).wait_send()
+
+            @pl.when(other != chip)
+            def _():
+                to_mate(slot, owner).wait_send()
+                for which in range(2):
+                    to_pair(slot, owner, which).wait_send()
+
+            @pl.when(other == chip)
+            def _():
+                shard_to_pair(slot, whole_shard(slot), owner).wait_send()
 
         return carry
 
@@ -407,31 +602,47 @@
     def kernel(*refs):
         stage_kernel(segments, places, layer_total, *refs)
 
-    vmem = pl.BlockSpec(memory_space=pltpu.VMEM)
+    anywhere = pl.BlockSpec(memory_space=pl.ANY)
+    half = jnp.bfloat16
     return pl.pallas_call(
         kernel,
-        out_shape=jax.ShapeDtypeStruct((kept, batches * rows, width), jnp.bfloat16),
-        in_specs=[vmem, pl.BlockSpec(memory_space=pl.ANY)] + [vmem] * 6,
-        out_specs=vmem,
+        out_shape=jax.ShapeDtypeStruct((kept, batches * rows, width), half),
+        in_specs=[anywhere] * 8,
+        out_specs=anywhere,
         scratch_shapes=[
-            pltpu.VMEM((kept, places * shard, width), jnp.bfloat16),
+            pltpu.VMEM(features.shape, half),
+            pltpu.VMEM((kept,) + history.shape[1:], half),
+            pltpu.VMEM(own_adj.shape, half),
+            pltpu.VMEM((batches, edges, rows), half),
+            pltpu.VMEM(hist_adj.shape, half),
+            pltpu.VMEM(send_ids.shape, send_ids.dtype),
+            pltpu.VMEM(hist_ids.shape, hist_ids.dtype),
+            pltpu.VMEM((kept, batches * rows, width), half),
+            pltpu.VMEM((2, kept, places * shard, width), half),
             pltpu.VMEM((kept, batches, rows, width), jnp.float32),
-            pltpu.VMEM((batches, edges, rows), jnp.bfloat16),
-            pltpu.VMEM((batches, rows, width), jnp.bfloat16),
-            pltpu.VMEM((kept, batches, edges, width), jnp.bfloat16),
-            pltpu.VMEM((kept, batches, edges, width), jnp.bfloat16),
+            pltpu.VMEM((batches, edges, rows), half),
+            pltpu.VMEM((batches, rows, width), half),
+            pltpu.VMEM((kept, batches, edges, width), half),
+            pltpu.VMEM((kept, batches, edges, width), half),
+            dma((7,)),
             dma((kept,)),
-            dma((kept, places)),
+            dma((kept, batches)),
+            dma((2, kept, chips)),
             dma((kept, chips)),
+            dma((kept, 2, chips)),
+            dma((kept,)),
+            dma((2, kept, chips)),
+            dma((2, kept, chips)),
             dma((kept, chips)),
-            dma((kept, chips)),
+            dma((kept, 2, chips)),
+            dma((kept,)),
             dma((kept, batches, len(OFFSETS))),
             dma((kept, batches, len(OFFSETS))),
             dma((batches,)),
             dma((batches,)),
         ],
         compiler_params=pltpu.CompilerParams(
-            collective_id=0, has_side_effects=True, vmem_limit_bytes=40 * 1024 * 1024
+            collective_id=0, has_side_effects=True, vmem_limit_bytes=60 * 1024 * 1024
         ),
     )(
         features,
@@ -446,9 +657,10 @@
 
 
 def device_part(features, weights, *rest):
-    places = lax.axis_size("graph")
-    whole_tiles = weights.shape[1] % TILE_ROWS == 0 and rest[2].shape[2] % TILE_ROWS == 0
-    if whole_tiles and places % 2 == 0 and weights.shape[0] % lax.axis_size("segment") == 0:
+    places, segments = lax.axis_size("graph"), lax.axis_size("segment")
+    whole_tiles = weights.shape[1] % (2 * TILE_ROWS) == 0 and rest[2].shape[2] % TILE_ROWS == 0
+    even = places % 2 == 0 and segments % 2 == 0 and weights.shape[0] % segments == 0
+    if whole_tiles and even:
         return staged(features, weights, *rest)
     return shards(features, weights, *rest)
 

time: 124 us -> 131 us (1.056)
  Pallas kernels: 114 us -> 127 us
  local copies, waits for them, and re-layouts: 9.32 us -> 3.08 us
    pallas_call x1, Pallas kernels: 114 us -> 127 us  [staged(): pl.pallas_call(kernel, out_shape=jax.ShapeDtypeStruct((kept, batches * ro...]
    unnamed x17 -> x1, local copies, waits for them, and re-layouts: 9.32 us -> 3.08 us
where the time goes in v2:
time: 131 us
  Pallas kernels  127 us (97%)
  local copies, waits for them, and re-layouts  3.08 us (2%)
    pallas_call x1, Pallas kernels, staged(): pl.pallas_call(kernel, out_shape=jax.ShapeDtypeStruct((kept, batches * ro...  127 us
    unnamed x1, local copies, waits for them, and re-layouts  3.08 us

profile of v2, /device:TPU:6, one launch (start us, length us, event | category | flops | bytes accessed | tf_op | source)
XLA Modules:
  0.0 130.6 jit_solution(16389324026319303358)
XLA Ops:
  0.0 127.5 %shard_map.82 = bf16[2,512,1024]{2,1,0:T(8,128)(2,1)} custom-call(bf16[512,1024]{1,0:T(8,128)(2,1)} %refs_0_.1, bf16[8,128,1024]{2,1,0:T(8,128)(2,1)} %refs_1_.1, bf16[8,64,1024]{2,1,0:T(8,128)(2,1)} %refs_2_.1, bf16[4,128,128]{2,1,0:T(8,128)(2,1)} %refs_3_.1, bf16[4,64,128]{2,1,0:T(8,128)(2,1)} %bitcast.1, bf16[4,64,128]{2,1,0:T(8,128)(2,1)} %refs_5_.1, ...), custom_call_target="tpu_custom_call" | custom-call | tf_op jit(solution)/shard_map/pallas_call | solution.py:607
  127.5 3.1 %copy.10 = bf16[2,512,1024]{2,1,0:T(8,128)(2,1)} copy(bf16[2,512,1024]{2,1,0:T(8,128)(2,1)} %shard_map.82) | data formatting | bytes 4194304

commit v3 on v2

--- a/solution.py
+++ b/solution.py
@@ -119,9 +119,9 @@
     features_in, weights, history_in, own_in, side_in, hist_in, send_in, ids_in,
     out,
     features, history, own_adj, side_adj, hist_adj, send_ids, hist_ids,
-    made, full, base, select, entering, leaving, arrived,
-    load_sem, own_sem, store_sem, line_recv, mate_recv, pair_recv, shard_recv,
-    up_send, down_send, mate_send, pair_send, shard_send,
+    full, base, select, entering, leaving, arrived,
+    load_sem, own_sem, line_recv, mate_recv, pair_recv, shard_recv,
+    up_send, down_send, line_send, mate_send, pair_send, shard_send,
     edge_send, edge_recv, hop_send, hop_recv,
 ):
     seg = lax.axis_index("segment")
@@ -210,10 +210,16 @@
     def held(turn, slot, owner, which):
         return full.at[turn, slot, piece_rows(owner, which)]
 
-    def along(turn, slot, source, owner, step, send_sem):
+    def along(slot, source, owner, step, send_sem):
         return push(
-            turn, slot, source, owner, side, {"graph": me + 2 * step},
-            send_sem.at[turn, slot, owner // 2], line_recv.at[turn, slot, owner // 2],
+            0, slot, source, owner, side, {"graph": me + 2 * step},
+            send_sem.at[slot, owner // 2], line_recv.at[0, slot, owner // 2],
+        )
+
+    def direct(slot, source, owner, target):
+        return push(
+            1, slot, source, owner, side, {"graph": target},
+            line_send.at[slot, target // 2], line_recv.at[1, slot, owner // 2],
         )
 
     def to_pair(slot, owner, which):
@@ -246,23 +252,42 @@
             device_id_type=MESH,
         )
 
-    def open_slot(turn, slot):
+    def half_shard(turn, slot):
         number = (seg + (turn - side) * half) * kept + slot
-        source = weights.at[number, pl.ds(pl.multiple_of(side * piece, piece), piece)]
-
-        @pl.when(chip < chips - 1)
-        def _():
-            along(turn, slot, source, me, 1, up_send).start()
-
-        @pl.when(chip > 0)
-        def _():
-            along(turn, slot, source, me, -1, down_send).start()
-
+        return weights.at[number, pl.ds(pl.multiple_of(side * piece, piece), piece)]
+
+    def place_own(turn, slot):
         @pl.when(side == turn)
         def _():
             shard_to_pair(slot, whole_shard(slot), me).start()
             own_copy(slot).start()
 
+    def open_slot(slot):
+        source = half_shard(0, slot)
+
+        @pl.when(chip < chips - 1)
+        def _():
+            along(slot, source, me, 1, up_send).start()
+
+        @pl.when(chip > 0)
+        def _():
+            along(slot, source, me, -1, down_send).start()
+
+        place_own(0, slot)
+
+    def around(distance, action):
+        for owner in (me - 2 * distance, me + 2 * distance):
+
+            @pl.when(jnp.logical_and(owner >= 0, owner < places))
+            def _():
+                action(owner)
+
+    def open_second(slot):
+        source = half_shard(1, slot)
+        for distance in range(1, chips):
+            around(distance, lambda target: direct(slot, source, me, target).start())
+        place_own(1, slot)
+
     def hand_on(turn, slot, owner):
         @pl.when(side == turn)
         def _():
@@ -272,32 +297,40 @@
         def _():
             to_mate(slot, owner).start()
 
-    def relay(turn, slot, distance):
+    def relay(slot, distance):
         below = me - 2 * distance
 
         @pl.when(below >= 0)
         def _():
-            block = held(turn, slot, below, side)
-            along(turn, slot, block, below, 1, up_send).wait_recv()
+            block = held(0, slot, below, side)
+            along(slot, block, below, 1, up_send).wait_recv()
 
             @pl.when(chip < chips - 1)
             def _():
-                along(turn, slot, block, below, 1, up_send).start()
-
-            hand_on(turn, slot, below)
+                along(slot, block, below, 1, up_send).start()
+
+            hand_on(0, slot, below)
 
         above = me + 2 * distance
 
         @pl.when(above < places)
         def _():
-            block = held(turn, slot, above, side)
-            along(turn, slot, block, above, -1, down_send).wait_recv()
+            block = held(0, slot, above, side)
+            along(slot, block, above, -1, down_send).wait_recv()
 
             @pl.when(chip > 0)
             def _():
-                along(turn, slot, block, above, -1, down_send).start()
-
-            hand_on(turn, slot, above)
+                along(slot, block, above, -1, down_send).start()
+
+            hand_on(0, slot, above)
+
+    def hand_second(slot):
+        def one(owner):
+            direct(slot, held(1, slot, owner, side), owner, owner).wait_recv()
+            hand_on(1, slot, owner)
+
+        for distance in range(1, chips):
+            around(distance, one)
 
     def bridge(slot, distance):
         for owner in (me - 2 * distance, me + 2 * distance):
@@ -354,16 +387,9 @@
     def batch_range(batch):
         return pl.ds(pl.multiple_of(batch * rows, rows), rows)
 
-    def store(slot, batch):
-        return pltpu.make_async_copy(
-            made.at[slot, batch_range(batch)],
-            out.at[slot, batch_range(batch)],
-            store_sem.at[slot, batch],
-        )
-
     def hop(batch):
         return pltpu.make_async_remote_copy(
-            src_ref=made.at[kept - 1, batch_range(batch)],
+            src_ref=out.at[kept - 1, batch_range(batch)],
             dst_ref=entering.at[batch],
             send_sem=hop_send.at[batch],
             recv_sem=hop_recv.at[batch],
@@ -408,7 +434,7 @@
         if slot == 0:
             current = entering[batch]
         else:
-            current = made[slot - 1, batch_range(batch), :]
+            current = out[slot - 1, batch_range(batch), :]
         aggregate = jnp.dot(own_adj[batch], current, preferred_element_type=jnp.float32)
         for direction in range(len(OFFSETS)):
 
@@ -423,8 +449,7 @@
         )
         result = jnp.maximum((1.0 - strength) * support + strength * mixing, 0.0)
         result = result.astype(jnp.bfloat16)
-        made[slot, batch_range(batch), :] = result
-        store(slot, batch).start()
+        out[slot, batch_range(batch), :] = result
         if slot < kept - 1:
             send_edges(slot + 1, batch, result)
         else:
@@ -435,71 +460,67 @@
 
     far = chips - 1
 
-    def line_steps(turn, slot):
-        steps = []
-        for distance in range(1, chips):
-            work = [(relay, (turn, slot, distance))]
-            if distance == max(1, far - 1):
-                if slot < kept - 1:
-                    work.append((open_slot, (turn, slot + 1)))
-                elif turn == 0:
-                    work.append((open_slot, (1, 0)))
-            steps.append(work)
-        return steps
-
-    def run(work):
-        for action, arguments in work:
-            action(*arguments)
-
     def bridges(slot):
         for distance in range(1, chips):
             bridge(slot, distance)
 
-    open_slot(0, 0)
+    def line_steps(slot):
+        steps = []
+        for distance in range(1, chips):
+            work = [(relay, (slot, distance))]
+            if distance == max(1, far - 1) and slot < kept - 1:
+                work.append((open_slot, (slot + 1,)))
+            if distance == far and slot == kept - 1:
+                work += [(open_second, (number,)) for number in range(kept)]
+            if distance > 1:
+                work.append((bridge, (slot, distance - 1)))
+            steps.append(work)
+        steps.append([(bridge, (slot, far))])
+        return steps
+
+    def run(work, bridging):
+        for action, arguments in work:
+            if action is not bridge:
+                action(*arguments)
+            elif bridging:
+
+                @pl.when(side == 0)
+                def _():
+                    action(*arguments)
+
+    open_slot(0)
     for load in loads:
         load.wait()
-    lax.fori_loop(0, batches, prepare, 0)
-    for work in line_steps(0, 0):
-        run(work)
-
-    @pl.when(side == 0)
+    middle = batches // 2
+    lax.fori_loop(0, middle, prepare, 0)
+    for number, work in enumerate(line_steps(0)):
+        run(work, True)
+        if number == 0:
+            lax.fori_loop(middle, batches, prepare, 0)
+
+            @pl.when(seg == 0)
+            def _():
+                def early(batch, carry):
+                    send_edges(0, batch, entering[batch])
+                    return carry
+
+                lax.fori_loop(0, batches, early, 0)
+
+    first_tasks = [[] for _ in range(batches * kept)]
+    for slot in range(1, kept):
+        for number, work in enumerate(line_steps(slot)):
+            first_tasks[min((slot - 1) * batches + number, slot * batches - 1)] += work
+
+    @pl.when(seg > 0)
     def _():
-        bridges(0)
-
-    last_first = batches * kept - 1
-    last_other = batches + kept - 2
-    first_tasks = [[] for _ in range(last_first + 1)]
-    other_tasks = [[] for _ in range(last_other + 1)]
-    later = []
-    for slot in range(1, kept):
-        steps = line_steps(0, slot)
-        for distance in range(1, chips):
-            if distance > 1:
-                steps[distance - 1].append((bridge, (slot, distance - 1)))
-        steps.append([(bridge, (slot, far))])
-        for number, work in enumerate(steps):
-            first_tasks[min((slot - 1) * batches + number, slot * batches - 1)] += work
-        later += steps
-    shared = []
-    for slot in range(kept):
-        shared += line_steps(1, slot)
-    for number, work in enumerate(shared):
-        first_tasks[min((kept - 1) * batches + number, last_first)] += work
-    for number, work in enumerate(shared[far:]):
-        other_tasks[min(number, last_other)] += work
-
-    @pl.when(jnp.logical_and(seg > 0, side == 0))
-    def _():
-        for work in later + shared[:far]:
-            run(work)
+        for slot in range(1, kept):
+            for work in line_steps(slot):
+                run(work, True)
 
     @pl.when(side == 1)
     def _():
-        for slot in range(1, kept):
-            for work in line_steps(0, slot):
-                run(work)
-        for work in shared:
-            run(work)
+        for slot in range(kept):
+            hand_second(slot)
         for slot in range(kept):
             bridges(slot)
 
@@ -507,19 +528,17 @@
     ticks = batches + lag * (kept - 1)
 
     def tick(time, carry):
-        @pl.when(time < batches)
-        def _():
-            @pl.when(seg > 0)
-            def _():
-                hop(time).wait_recv()
-
+        @pl.when(jnp.logical_and(seg > 0, time < batches))
+        def _():
+            hop(time).wait_recv()
             send_edges(0, time, entering[time])
 
         for number, work in enumerate(first_tasks):
-
-            @pl.when(jnp.logical_and(seg == 0, time == number))
-            def _():
-                run(work)
+            if work:
+
+                @pl.when(jnp.logical_and(seg == 0, time == number))
+                def _():
+                    run(work, True)
 
         for slot in range(kept - 1, -1, -1):
 
@@ -533,19 +552,28 @@
             def _():
                 layer(slot, batch)
 
-        for number, work in enumerate(other_tasks):
-
-            @pl.when(jnp.logical_and(jnp.logical_and(seg > 0, side == 0), time == number))
-            def _():
-                run(work)
+        for slot in range(kept):
+
+            @pl.when(
+                jnp.logical_and(
+                    jnp.logical_and(seg > 0, side == 0),
+                    time == min(2 * slot + 1, batches + kept - 2),
+                )
+            )
+            def _():
+                hand_second(slot)
 
         return carry
 
     lax.fori_loop(0, ticks, tick, 0)
+
+    @pl.when(seg == 0)
+    def _():
+        for slot in range(kept):
+            hand_second(slot)
 
     def finish(batch, carry):
         for slot in range(kept):
-            store(slot, batch).wait()
             for direction in range(len(OFFSETS)):
 
                 @pl.when(sends(direction))
@@ -563,19 +591,19 @@
     def drain(other, carry):
         owner = 2 * other + core
         for slot in range(kept):
-            for turn in range(2):
-                block = held(turn, slot, owner, side)
-
-                @pl.when(jnp.logical_and(other <= chip, chip < chips - 1))
-                def _():
-                    along(turn, slot, block, owner, 1, up_send).wait_send()
-
-                @pl.when(jnp.logical_and(other >= chip, chip > 0))
-                def _():
-                    along(turn, slot, block, owner, -1, down_send).wait_send()
+            block = held(0, slot, owner, side)
+
+            @pl.when(jnp.logical_and(other <= chip, chip < chips - 1))
+            def _():
+                along(slot, block, owner, 1, up_send).wait_send()
+
+            @pl.when(jnp.logical_and(other >= chip, chip > 0))
+            def _():
+                along(slot, block, owner, -1, down_send).wait_send()
 
             @pl.when(other != chip)
             def _():
+                direct(slot, half_shard(1, slot), me, owner).wait_send()
                 to_mate(slot, owner).wait_send()
                 for which in range(2):
                     to_pair(slot, owner, which).wait_send()
@@ -608,7 +636,7 @@
         kernel,
         out_shape=jax.ShapeDtypeStruct((kept, batches * rows, width), half),
         in_specs=[anywhere] * 8,
-        out_specs=anywhere,
+        out_specs=pl.BlockSpec(memory_space=pltpu.VMEM),
         scratch_shapes=[
             pltpu.VMEM(features.shape, half),
             pltpu.VMEM((kept,) + history.shape[1:], half),
@@ -617,7 +645,6 @@
             pltpu.VMEM(hist_adj.shape, half),
             pltpu.VMEM(send_ids.shape, send_ids.dtype),
             pltpu.VMEM(hist_ids.shape, hist_ids.dtype),
-            pltpu.VMEM((kept, batches * rows, width), half),
             pltpu.VMEM((2, kept, places * shard, width), half),
             pltpu.VMEM((kept, batches, rows, width), jnp.float32),
             pltpu.VMEM((batches, edges, rows), half),
@@ -626,13 +653,13 @@
             pltpu.VMEM((kept, batches, edges, width), half),
             dma((7,)),
             dma((kept,)),
-            dma((kept, batches)),
             dma((2, kept, chips)),
             dma((kept, chips)),
             dma((kept, 2, chips)),
             dma((kept,)),
-            dma((2, kept, chips)),
-            dma((2, kept, chips)),
+            dma((kept, chips)),
+            dma((kept, chips)),
+            dma((kept, chips)),
             dma((kept, chips)),
             dma((kept, 2, chips)),
             dma((kept,)),

time: 131 us -> 138 us (1.053)
  Pallas kernels: 127 us -> 135 us
    pallas_call x1, Pallas kernels: 127 us -> 135 us  [staged(): pl.pallas_call(kernel, out_shape=jax.ShapeDtypeStruct((kept, batches * ro...]
where the time goes in v3:
time: 138 us
  Pallas kernels  135 us (98%)
  local copies, waits for them, and re-layouts  3.08 us (2%)
    pallas_call x1, Pallas kernels, staged(): pl.pallas_call(kernel, out_shape=jax.ShapeDtypeStruct((kept, batches * ro...  135 us
    unnamed x1, local copies, waits for them, and re-layouts  3.08 us

profile of v3, /device:TPU:6, one launch (start us, length us, event | category | flops | bytes accessed | tf_op | source)
XLA Modules:
  0.0 137.7 jit_solution(7067068403615295560)
XLA Ops:
  0.0 134.6 %shard_map.82 = bf16[2,512,1024]{2,1,0:T(8,128)(2,1)} custom-call(bf16[512,1024]{1,0:T(8,128)(2,1)} %refs_0_.1, bf16[8,128,1024]{2,1,0:T(8,128)(2,1)} %refs_1_.1, bf16[8,64,1024]{2,1,0:T(8,128)(2,1)} %refs_2_.1, bf16[4,128,128]{2,1,0:T(8,128)(2,1)} %refs_3_.1, bf16[4,64,128]{2,1,0:T(8,128)(2,1)} %bitcast.1, bf16[4,64,128]{2,1,0:T(8,128)(2,1)} %refs_5_.1, ...), custom_call_target="tpu_custom_call" | custom-call | tf_op jit(solution)/shard_map/pallas_call | solution.py:635
  134.6 3.1 %copy.10 = bf16[2,512,1024]{2,1,0:T(8,128)(2,1)} copy(bf16[2,512,1024]{2,1,0:T(8,128)(2,1)} %shard_map.82) | data formatting | bytes 4194304

commit v4 on v3

--- a/solution.py
+++ b/solution.py
@@ -121,7 +121,7 @@
     features, history, own_adj, side_adj, hist_adj, send_ids, hist_ids,
     full, base, select, entering, leaving, arrived,
     load_sem, own_sem, line_recv, mate_recv, pair_recv, shard_recv,
-    up_send, down_send, line_send, mate_send, pair_send, shard_send,
+    up_send, down_send, up_whole, down_whole, mate_send, pair_send, shard_send,
     edge_send, edge_recv, hop_send, hop_recv,
 ):
     seg = lax.axis_index("segment")
@@ -216,10 +216,25 @@
             send_sem.at[slot, owner // 2], line_recv.at[0, slot, owner // 2],
         )
 
-    def direct(slot, source, owner, target):
-        return push(
-            1, slot, source, owner, side, {"graph": target},
-            line_send.at[slot, target // 2], line_recv.at[1, slot, owner // 2],
+    def along_whole(slot, source, owner, step, send_sem):
+        return pltpu.make_async_remote_copy(
+            src_ref=source,
+            dst_ref=full.at[1, slot, shard_rows(owner)],
+            send_sem=send_sem.at[slot, owner // 2],
+            recv_sem=line_recv.at[1, slot, owner // 2],
+            device_id={"graph": me + 2 * step},
+            device_id_type=MESH,
+        )
+
+    def whole_to_pair(slot, owner):
+        block = full.at[1, slot, shard_rows(owner)]
+        return pltpu.make_async_remote_copy(
+            src_ref=block,
+            dst_ref=block,
+            send_sem=pair_send.at[slot, 0, owner // 2],
+            recv_sem=pair_recv.at[slot, 0, owner // 2],
+            device_id={"graph": pair},
+            device_id_type=MESH,
         )
 
     def to_pair(slot, owner, which):
@@ -275,18 +290,45 @@
 
         place_own(0, slot)
 
-    def around(distance, action):
-        for owner in (me - 2 * distance, me + 2 * distance):
-
-            @pl.when(jnp.logical_and(owner >= 0, owner < places))
-            def _():
-                action(owner)
-
-    def open_second(slot):
-        source = half_shard(1, slot)
-        for distance in range(1, chips):
-            around(distance, lambda target: direct(slot, source, me, target).start())
+    def open_whole(slot):
+        source = whole_shard(slot)
+
+        @pl.when(chip < chips - 1)
+        def _():
+            along_whole(slot, source, me, 1, up_whole).start()
+
+        @pl.when(chip > 0)
+        def _():
+            along_whole(slot, source, me, -1, down_whole).start()
+
         place_own(1, slot)
+
+    def relay_whole(slot, distance):
+        below = me - 2 * distance
+
+        @pl.when(below >= 0)
+        def _():
+            block = full.at[1, slot, shard_rows(below)]
+            along_whole(slot, block, below, 1, up_whole).wait_recv()
+
+            @pl.when(chip < chips - 1)
+            def _():
+                along_whole(slot, block, below, 1, up_whole).start()
+
+            whole_to_pair(slot, below).start()
+
+        above = me + 2 * distance
+
+        @pl.when(above < places)
+        def _():
+            block = full.at[1, slot, shard_rows(above)]
+            along_whole(slot, block, above, -1, down_whole).wait_recv()
+
+            @pl.when(chip > 0)
+            def _():
+                along_whole(slot, block, above, -1, down_whole).start()
+
+            whole_to_pair(slot, above).start()
 
     def hand_on(turn, slot, owner):
         @pl.when(side == turn)
@@ -323,14 +365,6 @@
                 along(slot, block, above, -1, down_send).start()
 
             hand_on(0, slot, above)
-
-    def hand_second(slot):
-        def one(owner):
-            direct(slot, held(1, slot, owner, side), owner, owner).wait_recv()
-            hand_on(1, slot, owner)
-
-        for distance in range(1, chips):
-            around(distance, one)
 
     def bridge(slot, distance):
         for owner in (me - 2 * distance, me + 2 * distance):
@@ -348,8 +382,15 @@
             @pl.when(other != chip)
             def _():
                 owner = 2 * other + 1 - core
-                for which in range(2):
-                    to_pair(slot, owner, which).wait_recv()
+
+                @pl.when(side == 0)
+                def _():
+                    for which in range(2):
+                        to_pair(slot, owner, which).wait_recv()
+
+                @pl.when(side == 1)
+                def _():
+                    whole_to_pair(slot, owner).wait_recv()
 
             return carry
 
@@ -460,33 +501,28 @@
 
     far = chips - 1
 
-    def bridges(slot):
-        for distance in range(1, chips):
-            bridge(slot, distance)
-
     def line_steps(slot):
         steps = []
         for distance in range(1, chips):
             work = [(relay, (slot, distance))]
             if distance == max(1, far - 1) and slot < kept - 1:
                 work.append((open_slot, (slot + 1,)))
-            if distance == far and slot == kept - 1:
-                work += [(open_second, (number,)) for number in range(kept)]
             if distance > 1:
                 work.append((bridge, (slot, distance - 1)))
             steps.append(work)
         steps.append([(bridge, (slot, far))])
         return steps
 
-    def run(work, bridging):
+    def run(work):
         for action, arguments in work:
-            if action is not bridge:
+            if action is bridge:
+
+                @pl.when(side == 0)
+                def _():
+                    action(*arguments)
+
+            else:
                 action(*arguments)
-            elif bridging:
-
-                @pl.when(side == 0)
-                def _():
-                    action(*arguments)
 
     open_slot(0)
     for load in loads:
@@ -494,7 +530,9 @@
     middle = batches // 2
     lax.fori_loop(0, middle, prepare, 0)
     for number, work in enumerate(line_steps(0)):
-        run(work, True)
+        if number == far and kept > 1:
+            relay(1, 1)
+        run(work)
         if number == 0:
             lax.fori_loop(middle, batches, prepare, 0)
 
@@ -507,22 +545,35 @@
                 lax.fori_loop(0, batches, early, 0)
 
     first_tasks = [[] for _ in range(batches * kept)]
+    others = []
     for slot in range(1, kept):
-        for number, work in enumerate(line_steps(slot)):
+        steps = line_steps(slot)
+        if slot == 1:
+            steps[0] = steps[0][1:]
+            steps = [steps[0] + steps[1]] + steps[2:] if far > 1 else steps
+        others += steps
+        for number, work in enumerate(steps):
             first_tasks[min((slot - 1) * batches + number, slot * batches - 1)] += work
 
     @pl.when(seg > 0)
     def _():
-        for slot in range(1, kept):
-            for work in line_steps(slot):
-                run(work, True)
+        for number, work in enumerate(others):
+            run(work)
+            if number == 0:
+
+                @pl.when(side == 1)
+                def _():
+                    open_whole(0)
 
     @pl.when(side == 1)
     def _():
+        if not others:
+            open_whole(0)
         for slot in range(kept):
-            hand_second(slot)
-        for slot in range(kept):
-            bridges(slot)
+            for distance in range(1, chips):
+                relay_whole(slot, distance)
+                if slot < kept - 1 and distance == max(1, far - 1):
+                    open_whole(slot + 1)
 
     lag = jnp.where(seg == 0, batches, 1)
     ticks = batches + lag * (kept - 1)
@@ -538,7 +589,7 @@
 
                 @pl.when(jnp.logical_and(seg == 0, time == number))
                 def _():
-                    run(work, True)
+                    run(work)
 
         for slot in range(kept - 1, -1, -1):
 
@@ -552,25 +603,9 @@
             def _():
                 layer(slot, batch)
 
-        for slot in range(kept):
-
-            @pl.when(
-                jnp.logical_and(
-                    jnp.logical_and(seg > 0, side == 0),
-                    time == min(2 * slot + 1, batches + kept - 2),
-                )
-            )
-            def _():
-                hand_second(slot)
-
         return carry
 
     lax.fori_loop(0, ticks, tick, 0)
-
-    @pl.when(seg == 0)
-    def _():
-        for slot in range(kept):
-            hand_second(slot)
 
     def finish(batch, carry):
         for slot in range(kept):
@@ -597,16 +632,29 @@
             def _():
                 along(slot, block, owner, 1, up_send).wait_send()
 
+                @pl.when(side == 1)
+                def _():
+                    along_whole(slot, whole_shard(slot), owner, 1, up_whole).wait_send()
+
             @pl.when(jnp.logical_and(other >= chip, chip > 0))
             def _():
                 along(slot, block, owner, -1, down_send).wait_send()
 
+                @pl.when(side == 1)
+                def _():
+                    along_whole(slot, whole_shard(slot), owner, -1, down_whole).wait_send()
+
             @pl.when(other != chip)
             def _():
-                direct(slot, half_shard(1, slot), me, owner).wait_send()
-                to_mate(slot, owner).wait_send()
-                for which in range(2):
-                    to_pair(slot, owner, which).wait_send()
+                @pl.when(side == 0)
+                def _():
+                    for which in range(2):
+                        to_pair(slot, owner, which).wait_send()
+
+                @pl.when(side == 1)
+                def _():
+                    to_mate(slot, owner).wait_send()
+                    whole_to_pair(slot, owner).wait_send()
 
             @pl.when(other == chip)
             def _():
@@ -661,6 +709,7 @@
             dma((kept, chips)),
             dma((kept, chips)),
             dma((kept, chips)),
+            dma((kept, chips)),
             dma((kept, 2, chips)),
             dma((kept,)),
             dma((kept, batches, len(OFFSETS))),

time: 138 us -> 105 us (0.76)
  Pallas kernels: 135 us -> 101 us
    pallas_call x1, Pallas kernels: 135 us -> 101 us  [staged(): pl.pallas_call(kernel, out_shape=jax.ShapeDtypeStruct((kept, batches * ro...]
where the time goes in v4:
time: 105 us; the launch traced here: 104 us
  Pallas kernels  101 us (96%)
  local copies, waits for them, and re-layouts  3.08 us (3%)
    pallas_call x1, Pallas kernels, staged(): pl.pallas_call(kernel, out_shape=jax.ShapeDtypeStruct((kept, batches * ro...  101 us
    unnamed x1, local copies, waits for them, and re-layouts  3.08 us

profile of v4, /device:TPU:6, one launch (start us, length us, event | category | flops | bytes accessed | tf_op | source)
XLA Modules:
  0.0 104.4 jit_solution(4414416902487486172)
XLA Ops:
  0.0 101.4 %shard_map.82 = bf16[2,512,1024]{2,1,0:T(8,128)(2,1)} custom-call(bf16[512,1024]{1,0:T(8,128)(2,1)} %refs_0_.1, bf16[8,128,1024]{2,1,0:T(8,128)(2,1)} %refs_1_.1, bf16[8,64,1024]{2,1,0:T(8,128)(2,1)} %refs_2_.1, bf16[4,128,128]{2,1,0:T(8,128)(2,1)} %refs_3_.1, bf16[4,64,128]{2,1,0:T(8,128)(2,1)} %bitcast.1, bf16[4,64,128]{2,1,0:T(8,128)(2,1)} %refs_5_.1, ...), custom_call_target="tpu_custom_call" | custom-call | tf_op jit(solution)/shard_map/pallas_call | solution.py:683
  101.4 3.1 %copy.10 = bf16[2,512,1024]{2,1,0:T(8,128)(2,1)} copy(bf16[2,512,1024]{2,1,0:T(8,128)(2,1)} %shard_map.82) | data formatting | bytes 4194304

commit v5 on v4

--- a/solution.py
+++ b/solution.py
@@ -92,6 +92,8 @@
 
 
 TILE_ROWS = 16
+TILE_COLUMNS = 128
+HALVES = 2
 MESH = pl.DeviceIdType.MESH
 
 
@@ -396,13 +398,18 @@
 
         lax.fori_loop(0, chips, from_pair, 0)
 
-    def edge_copy(slot, batch, direction):
+    wide = features.shape[1] // HALVES
+
+    def columns(part):
+        return pl.ds(part * wide, wide)
+
+    def edge_copy(slot, batch, direction, half_at):
         part = pl.ds(direction * edge, edge)
         return pltpu.make_async_remote_copy(
-            src_ref=leaving.at[slot, batch, part],
-            dst_ref=arrived.at[slot, batch, part],
-            send_sem=edge_send.at[slot, batch, direction],
-            recv_sem=edge_recv.at[slot, batch, direction],
+            src_ref=leaving.at[slot, batch, part, columns(half_at)],
+            dst_ref=arrived.at[slot, batch, part, columns(half_at)],
+            send_sem=edge_send.at[slot, batch, direction, half_at],
+            recv_sem=edge_recv.at[slot, batch, direction, half_at],
             device_id={"graph": me + OFFSETS[direction]},
             device_id_type=MESH,
         )
@@ -415,25 +422,25 @@
         there = me - OFFSETS[direction]
         return jnp.logical_and(there >= 0, there < places)
 
-    def send_edges(slot, batch, current):
-        leaving[slot, batch] = jnp.dot(
+    def send_edges(slot, batch, half_at, current):
+        leaving[slot, batch, :, columns(half_at)] = jnp.dot(
             select[batch], current, preferred_element_type=jnp.float32
         ).astype(jnp.bfloat16)
         for direction in range(len(OFFSETS)):
 
             @pl.when(sends(direction))
             def _():
-                edge_copy(slot, batch, direction).start()
+                edge_copy(slot, batch, direction, half_at).start()
 
     def batch_range(batch):
         return pl.ds(pl.multiple_of(batch * rows, rows), rows)
 
-    def hop(batch):
+    def hop(batch, half_at):
         return pltpu.make_async_remote_copy(
-            src_ref=out.at[kept - 1, batch_range(batch)],
-            dst_ref=entering.at[batch],
-            send_sem=hop_send.at[batch],
-            recv_sem=hop_recv.at[batch],
+            src_ref=out.at[kept - 1, batch_range(batch), columns(half_at)],
+            dst_ref=entering.at[batch, :, columns(half_at)],
+            send_sem=hop_send.at[batch, half_at],
+            recv_sem=hop_recv.at[batch, half_at],
             device_id={"segment": seg + 1},
             device_id_type=MESH,
         )
@@ -472,32 +479,45 @@
         for number in range(layer_total):
             value = math.log(LAMBDA / (number + 1.0) + 1.0)
             strength = jnp.where(first_layer + slot == number, jnp.float32(value), strength)
-        if slot == 0:
-            current = entering[batch]
-        else:
-            current = out[slot - 1, batch_range(batch), :]
-        aggregate = jnp.dot(own_adj[batch], current, preferred_element_type=jnp.float32)
-        for direction in range(len(OFFSETS)):
-
-            @pl.when(receives(direction))
-            def _():
-                edge_copy(slot, batch, direction).wait_recv()
-
-        aggregate = aggregate + transposed_dot(side_adj[batch], arrived[slot, batch])
-        support = (1.0 - ALPHA) * aggregate + base[slot, batch]
-        mixing = jnp.dot(
-            support.astype(jnp.bfloat16), full[side, slot], preferred_element_type=jnp.float32
-        )
-        result = jnp.maximum((1.0 - strength) * support + strength * mixing, 0.0)
-        result = result.astype(jnp.bfloat16)
-        out[slot, batch_range(batch), :] = result
-        if slot < kept - 1:
-            send_edges(slot + 1, batch, result)
-        else:
-
-            @pl.when(seg < segments - 1)
-            def _():
-                hop(batch).start()
+        supports = []
+        mixing = [None] * HALVES
+        for part in range(HALVES):
+            if slot == 0:
+                current = entering[batch, :, columns(part)]
+            else:
+                current = out[slot - 1, batch_range(batch), columns(part)]
+            aggregate = jnp.dot(own_adj[batch], current, preferred_element_type=jnp.float32)
+            for direction in range(len(OFFSETS)):
+
+                @pl.when(receives(direction))
+                def _():
+                    edge_copy(slot, batch, direction, part).wait_recv()
+
+            aggregate = aggregate + transposed_dot(
+                side_adj[batch], arrived[slot, batch, :, columns(part)]
+            )
+            support = (1.0 - ALPHA) * aggregate + base[slot, batch, :, columns(part)]
+            supports.append(support)
+            rounded = support.astype(jnp.bfloat16)
+            for target in range(HALVES):
+                term = jnp.dot(
+                    rounded,
+                    full[side, slot, columns(part), columns(target)],
+                    preferred_element_type=jnp.float32,
+                )
+                mixing[target] = term if part == 0 else mixing[target] + term
+                if part < HALVES - 1:
+                    continue
+                mixed = (1.0 - strength) * supports[target] + strength * mixing[target]
+                result = jnp.maximum(mixed, 0.0).astype(jnp.bfloat16)
+                out[slot, batch_range(batch), columns(target)] = result
+                if slot < kept - 1:
+                    send_edges(slot + 1, batch, target, result)
+                else:
+
+                    @pl.when(seg < segments - 1)
+                    def _():
+                        hop(batch, target).start()
 
     far = chips - 1
 
@@ -539,7 +559,8 @@
             @pl.when(seg == 0)
             def _():
                 def early(batch, carry):
-                    send_edges(0, batch, entering[batch])
+                    for part in range(HALVES):
+                        send_edges(0, batch, part, entering[batch, :, columns(part)])
                     return carry
 
                 lax.fori_loop(0, batches, early, 0)
@@ -581,8 +602,9 @@
     def tick(time, carry):
         @pl.when(jnp.logical_and(seg > 0, time < batches))
         def _():
-            hop(time).wait_recv()
-            send_edges(0, time, entering[time])
+            for part in range(HALVES):
+                hop(time, part).wait_recv()
+                send_edges(0, time, part, entering[time, :, columns(part)])
 
         for number, work in enumerate(first_tasks):
             if work:
@@ -613,11 +635,13 @@
 
                 @pl.when(sends(direction))
                 def _():
-                    edge_copy(slot, batch, direction).wait_send()
+                    for part in range(HALVES):
+                        edge_copy(slot, batch, direction, part).wait_send()
 
         @pl.when(seg < segments - 1)
         def _():
-            hop(batch).wait_send()
+            for part in range(HALVES):
+                hop(batch, part).wait_send()
 
         return carry
 
@@ -678,12 +702,12 @@
     def kernel(*refs):
         stage_kernel(segments, places, layer_total, *refs)
 
-    anywhere = pl.BlockSpec(memory_space=pl.ANY)
+    stored = pl.BlockSpec(memory_space=pl.ANY)
     half = jnp.bfloat16
     return pl.pallas_call(
         kernel,
         out_shape=jax.ShapeDtypeStruct((kept, batches * rows, width), half),
-        in_specs=[anywhere] * 8,
+        in_specs=[stored] * 8,
         out_specs=pl.BlockSpec(memory_space=pltpu.VMEM),
         scratch_shapes=[
             pltpu.VMEM(features.shape, half),
@@ -712,10 +736,10 @@
             dma((kept, chips)),
             dma((kept, 2, chips)),
             dma((kept,)),
-            dma((kept, batches, len(OFFSETS))),
-            dma((kept, batches, len(OFFSETS))),
-            dma((batches,)),
-            dma((batches,)),
+            dma((kept, batches, len(OFFSETS), HALVES)),
+            dma((kept, batches, len(OFFSETS), HALVES)),
+            dma((batches, HALVES)),
+            dma((batches, HALVES)),
         ],
         compiler_params=pltpu.CompilerParams(
             collective_id=0, has_side_effects=True, vmem_limit_bytes=60 * 1024 * 1024
@@ -736,6 +760,7 @@
     places, segments = lax.axis_size("graph"), lax.axis_size("segment")
     whole_tiles = weights.shape[1] % (2 * TILE_ROWS) == 0 and rest[2].shape[2] % TILE_ROWS == 0
     even = places % 2 == 0 and segments % 2 == 0 and weights.shape[0] % segments == 0
+    whole_tiles = whole_tiles and features.shape[1] % (HALVES * TILE_COLUMNS) == 0
     if whole_tiles and even:
         return staged(features, weights, *rest)
     return shards(features, weights, *rest)

time: 105 us -> 106 us (level)
  no operation moved by 1% of the time
where the time goes in v5:
time: 106 us; the launch traced here: 105 us
  Pallas kernels  102 us (96%)
  local copies, waits for them, and re-layouts  3.08 us (3%)
    pallas_call x1, Pallas kernels, staged(): pl.pallas_call(kernel, out_shape=jax.ShapeDtypeStruct((kept, batches * ro...  102 us
    unnamed x1, local copies, waits for them, and re-layouts  3.08 us

profile of v5, /device:TPU:6, one launch (start us, length us, event | category | flops | bytes accessed | tf_op | source)
XLA Modules:
  0.0 105.4 jit_solution(6725803921525663745)
XLA Ops:
  0.0 102.3 %shard_map.82 = bf16[2,512,1024]{2,1,0:T(8,128)(2,1)} custom-call(bf16[512,1024]{1,0:T(8,128)(2,1)} %refs_0_.1, bf16[8,128,1024]{2,1,0:T(8,128)(2,1)} %refs_1_.1, bf16[8,64,1024]{2,1,0:T(8,128)(2,1)} %refs_2_.1, bf16[4,128,128]{2,1,0:T(8,128)(2,1)} %refs_3_.1, bf16[4,64,128]{2,1,0:T(8,128)(2,1)} %bitcast.1, bf16[4,64,128]{2,1,0:T(8,128)(2,1)} %refs_5_.1, ...), custom_call_target="tpu_custom_call" | custom-call | tf_op jit(solution)/shard_map/pallas_call | solution.py:707
  102.3 3.1 %copy.10 = bf16[2,512,1024]{2,1,0:T(8,128)(2,1)} copy(bf16[2,512,1024]{2,1,0:T(8,128)(2,1)} %shard_map.82) | data formatting | bytes 4194304

commit v6 on v4

--- a/solution.py
+++ b/solution.py
@@ -119,7 +119,7 @@
     features_in, weights, history_in, own_in, side_in, hist_in, send_in, ids_in,
     out,
     features, history, own_adj, side_adj, hist_adj, send_ids, hist_ids,
-    full, base, select, entering, leaving, arrived,
+    full, base, select, crossed, entering, leaving, arrived,
     load_sem, own_sem, line_recv, mate_recv, pair_recv, shard_recv,
     up_send, down_send, up_whole, down_whole, mate_send, pair_send, shard_send,
     edge_send, edge_recv, hop_send, hop_recv,
@@ -416,14 +416,16 @@
         return jnp.logical_and(there >= 0, there < places)
 
     def send_edges(slot, batch, current):
-        leaving[slot, batch] = jnp.dot(
-            select[batch], current, preferred_element_type=jnp.float32
-        ).astype(jnp.bfloat16)
+        both = jnp.dot(select[batch], current, preferred_element_type=jnp.float32)
+        edges = leaving.shape[2]
+        leaving[slot, batch] = both[:edges].astype(jnp.bfloat16)
         for direction in range(len(OFFSETS)):
 
             @pl.when(sends(direction))
             def _():
                 edge_copy(slot, batch, direction).start()
+
+        base[slot, batch] = base[slot, batch] + (1.0 - ALPHA) * both[edges:]
 
     def batch_range(batch):
         return pl.ds(pl.multiple_of(batch * rows, rows), rows)
@@ -452,6 +454,9 @@
                         (edge, arrived.shape[3]), jnp.bfloat16
                     )
 
+        edges = leaving.shape[2]
+        select[batch, pl.ds(edges, rows)] = own_adj[batch]
+        crossed[batch] = side_adj[batch].astype(jnp.float32).T.astype(jnp.bfloat16)
         initial = features[batch_range(batch), :]
 
         @pl.when(seg == 0)
@@ -472,19 +477,16 @@
         for number in range(layer_total):
             value = math.log(LAMBDA / (number + 1.0) + 1.0)
             strength = jnp.where(first_layer + slot == number, jnp.float32(value), strength)
-        if slot == 0:
-            current = entering[batch]
-        else:
-            current = out[slot - 1, batch_range(batch), :]
-        aggregate = jnp.dot(own_adj[batch], current, preferred_element_type=jnp.float32)
         for direction in range(len(OFFSETS)):
 
             @pl.when(receives(direction))
             def _():
                 edge_copy(slot, batch, direction).wait_recv()
 
-        aggregate = aggregate + transposed_dot(side_adj[batch], arrived[slot, batch])
-        support = (1.0 - ALPHA) * aggregate + base[slot, batch]
+        received = jnp.dot(
+            crossed[batch], arrived[slot, batch], preferred_element_type=jnp.float32
+        )
+        support = (1.0 - ALPHA) * received + base[slot, batch]
         mixing = jnp.dot(
             support.astype(jnp.bfloat16), full[side, slot], preferred_element_type=jnp.float32
         )
@@ -695,7 +697,8 @@
             pltpu.VMEM(hist_ids.shape, hist_ids.dtype),
             pltpu.VMEM((2, kept, places * shard, width), half),
             pltpu.VMEM((kept, batches, rows, width), jnp.float32),
-            pltpu.VMEM((batches, edges, rows), half),
+            pltpu.VMEM((batches, edges + rows, rows), half),
+            pltpu.VMEM((batches, rows, edges), half),
             pltpu.VMEM((batches, rows, width), half),
             pltpu.VMEM((kept, batches, edges, width), half),
             pltpu.VMEM((kept, batches, edges, width), half),

time: 105 us -> 104 us (level)
  no operation moved by 1% of the time
where the time goes in v6:
time: 104 us; the launch traced here: 103 us
  Pallas kernels  100 us (96%)
  local copies, waits for them, and re-layouts  3.08 us (3%)
    pallas_call x1, Pallas kernels, staged(): pl.pallas_call(kernel, out_shape=jax.ShapeDtypeStruct((kept, batches * ro...  100 us
    unnamed x1, local copies, waits for them, and re-layouts  3.08 us

profile of v6, /device:TPU:6, one launch (start us, length us, event | category | flops | bytes accessed | tf_op | source)
XLA Modules:
  0.0 103.4 jit_solution(9373089692218608012)
XLA Ops:
  0.0 100.3 %shard_map.82 = bf16[2,512,1024]{2,1,0:T(8,128)(2,1)} custom-call(bf16[512,1024]{1,0:T(8,128)(2,1)} %refs_0_.1, bf16[8,128,1024]{2,1,0:T(8,128)(2,1)} %refs_1_.1, bf16[8,64,1024]{2,1,0:T(8,128)(2,1)} %refs_2_.1, bf16[4,128,128]{2,1,0:T(8,128)(2,1)} %refs_3_.1, bf16[4,64,128]{2,1,0:T(8,128)(2,1)} %bitcast.1, bf16[4,64,128]{2,1,0:T(8,128)(2,1)} %refs_5_.1, ...), custom_call_target="tpu_custom_call" | custom-call | tf_op jit(solution)/shard_map/pallas_call | solution.py:685
  100.3 3.1 %copy.10 = bf16[2,512,1024]{2,1,0:T(8,128)(2,1)} copy(bf16[2,512,1024]{2,1,0:T(8,128)(2,1)} %shard_map.82) | data formatting | bytes 4194304

commit v7 on v6

--- a/solution.py
+++ b/solution.py
@@ -119,8 +119,8 @@
     features_in, weights, history_in, own_in, side_in, hist_in, send_in, ids_in,
     out,
     features, history, own_adj, side_adj, hist_adj, send_ids, hist_ids,
-    full, base, select, crossed, entering, leaving, arrived,
-    load_sem, own_sem, line_recv, mate_recv, pair_recv, shard_recv,
+    made, full, base, select, crossed, entering, leaving, arrived,
+    load_sem, own_sem, store_sem, line_recv, mate_recv, pair_recv, shard_recv,
     up_send, down_send, up_whole, down_whole, mate_send, pair_send, shard_send,
     edge_send, edge_recv, hop_send, hop_recv,
 ):
@@ -430,9 +430,16 @@
     def batch_range(batch):
         return pl.ds(pl.multiple_of(batch * rows, rows), rows)
 
+    def store(slot, batch):
+        return pltpu.make_async_copy(
+            made.at[slot, batch_range(batch)],
+            out.at[slot, batch_range(batch)],
+            store_sem.at[slot, batch],
+        )
+
     def hop(batch):
         return pltpu.make_async_remote_copy(
-            src_ref=out.at[kept - 1, batch_range(batch)],
+            src_ref=made.at[kept - 1, batch_range(batch)],
             dst_ref=entering.at[batch],
             send_sem=hop_send.at[batch],
             recv_sem=hop_recv.at[batch],
@@ -492,7 +499,8 @@
         )
         result = jnp.maximum((1.0 - strength) * support + strength * mixing, 0.0)
         result = result.astype(jnp.bfloat16)
-        out[slot, batch_range(batch), :] = result
+        made[slot, batch_range(batch), :] = result
+        store(slot, batch).start()
         if slot < kept - 1:
             send_edges(slot + 1, batch, result)
         else:
@@ -529,23 +537,27 @@
     open_slot(0)
     for load in loads:
         load.wait()
-    middle = batches // 2
-    lax.fori_loop(0, middle, prepare, 0)
+
+    def ready(batch, carry):
+        prepare(batch, carry)
+
+        @pl.when(seg == 0)
+        def _():
+            send_edges(0, batch, entering[batch])
+
+        return carry
+
+    def make_ready(share):
+        low, high = batches * share // (far + 1), batches * (share + 1) // (far + 1)
+        lax.fori_loop(low, high, ready, 0)
+
+    make_ready(0)
     for number, work in enumerate(line_steps(0)):
         if number == far and kept > 1:
             relay(1, 1)
         run(work)
-        if number == 0:
-            lax.fori_loop(middle, batches, prepare, 0)
-
-            @pl.when(seg == 0)
-            def _():
-                def early(batch, carry):
-                    send_edges(0, batch, entering[batch])
-                    return carry
-
-                lax.fori_loop(0, batches, early, 0)
-
+        if number < far:
+            make_ready(number + 1)
     first_tasks = [[] for _ in range(batches * kept)]
     others = []
     for slot in range(1, kept):
@@ -611,6 +623,7 @@
 
     def finish(batch, carry):
         for slot in range(kept):
+            store(slot, batch).wait()
             for direction in range(len(OFFSETS)):
 
                 @pl.when(sends(direction))
@@ -686,7 +699,7 @@
         kernel,
         out_shape=jax.ShapeDtypeStruct((kept, batches * rows, width), half),
         in_specs=[anywhere] * 8,
-        out_specs=pl.BlockSpec(memory_space=pltpu.VMEM),
+        out_specs=anywhere,
         scratch_shapes=[
             pltpu.VMEM(features.shape, half),
             pltpu.VMEM((kept,) + history.shape[1:], half),
@@ -695,6 +708,7 @@
             pltpu.VMEM(hist_adj.shape, half),
             pltpu.VMEM(send_ids.shape, send_ids.dtype),
             pltpu.VMEM(hist_ids.shape, hist_ids.dtype),
+            pltpu.VMEM((kept, batches * rows, width), half),
             pltpu.VMEM((2, kept, places * shard, width), half),
             pltpu.VMEM((kept, batches, rows, width), jnp.float32),
             pltpu.VMEM((batches, edges + rows, rows), half),
@@ -704,6 +718,7 @@
             pltpu.VMEM((kept, batches, edges, width), half),
             dma((7,)),
             dma((kept,)),
+            dma((kept, batches)),
             dma((2, kept, chips)),
             dma((kept, chips)),
             dma((kept, 2, chips)),

time: 104 us -> 103 us (level)
  no operation moved by 1% of the time
where the time goes in v7:
time: 103 us
  Pallas kernels  99.5 us (97%)
  local copies, waits for them, and re-layouts  3.08 us (3%)
    pallas_call x1, Pallas kernels, staged(): pl.pallas_call(kernel, out_shape=jax.ShapeDtypeStruct((kept, batches * ro...  99.5 us
    unnamed x1, local copies, waits for them, and re-layouts  3.08 us

profile of v7, /device:TPU:6, one launch (start us, length us, event | category | flops | bytes accessed | tf_op | source)
XLA Modules:
  0.0 102.6 jit_solution(3257420662712139446)
XLA Ops:
  0.0 99.5 %shard_map.82 = bf16[2,512,1024]{2,1,0:T(8,128)(2,1)} custom-call(bf16[512,1024]{1,0:T(8,128)(2,1)} %refs_0_.1, bf16[8,128,1024]{2,1,0:T(8,128)(2,1)} %refs_1_.1, bf16[8,64,1024]{2,1,0:T(8,128)(2,1)} %refs_2_.1, bf16[4,128,128]{2,1,0:T(8,128)(2,1)} %refs_3_.1, bf16[4,64,128]{2,1,0:T(8,128)(2,1)} %bitcast.1, bf16[4,64,128]{2,1,0:T(8,128)(2,1)} %refs_5_.1, ...), custom_call_target="tpu_custom_call" | custom-call | tf_op jit(solution)/shard_map/pallas_call | solution.py:698
  99.5 3.1 %copy.10 = bf16[2,512,1024]{2,1,0:T(8,128)(2,1)} copy(bf16[2,512,1024]{2,1,0:T(8,128)(2,1)} %shard_map.82) | data formatting | bytes 4194304
